TPU v7x, 32 devices: a whole 2x2x4 slice. The times are simulated.
32 devices in a mesh: groups: 2 (over x), branch: 16 (over z, y, core).
Axes of the slice: x: 2, y: 2, z: 4, core: 2. Of those that a mesh axis runs over, the one named last changes fastest.
Arguments:
- xbc: bfloat16 [8192, 8448], P(('groups', 'branch')), parts along dimension 0, may hold values from -6 to 6
- step_size: float32 [8192, 64], P(('groups', 'branch')), parts along dimension 0, may hold values from 0.15 to 32, as said below
- queries: bfloat16 [8192, 4096], P(('groups', 'branch')), parts along dimension 0, may hold values from -80 to 80
- keys_values: bfloat16 [8192, 1024], P(('groups', 'branch')), parts along dimension 0, may hold values from -4 to 4
- parent_slot: int32 [32], P('groups'), parts along dimension 0, may hold values from 0 to 15, as said below
- decay_rate: float32 [64], replicated, may hold values from 0.0001 to 0.05, as said below
- skip_gain: float32 [64], replicated, may hold values from 0.1 to 1.9
- conv_weight: float32 [4, 8448], replicated, may hold values from -3 to 3
Outputs:
- ssm_out: bfloat16 [8192, 8192], P(('groups', 'branch')), parts along dimension 0
- attn_out: bfloat16 [8192, 4096], P(('groups', 'branch')), parts along dimension 0
There are 2 independent parts, one for each index of `groups`. A program takes and returns all parts, laid end to end along the dimension named above; an argument that names none is the same for every part. Nothing has to cross between parts.
Inputs may be any that keep to these rules, and one draw needn't show every extreme that they name: parent_slot[i] == i exactly when slot i holds a root, and 2 slots do; exactly 6 slots have a root as parent, and every other slot has a parent whose parent is a root; the first and the last slot hold roots. `step_size`: positive. `decay_rate`: positive.
All inputs are finite; a program needn't handle non-finite values.
Results may differ from a plain program's by a relative error of at most 0.0048.
Values may be sent and summed in bfloat16 or wider, within the bound.
A program may use at most 128 MiB of HBM per device.

v0:
```python
import jax
import jax.numpy as jnp
from jax import lax
from jax.sharding import PartitionSpec as P

SSM_HEADS = 64
HEAD_DIM = 128
STATE_DIM = 128
Q_HEADS = 32
KV_HEADS = 4
ATT_DIM = 128
WINDOW = 512


EPSILON = 1e-05


def to_rows(flat_vec, device_count):
    return flat_vec.reshape(device_count, -1)


def from_rows(row_block, target_shape):
    return row_block.reshape(-1).reshape(target_shape)


def forward_only_filter(raw_rows, tail_rows, conv_weight):
    joined = jnp.concatenate([tail_rows, raw_rows], axis=0).astype(jnp.float32)
    length = raw_rows.shape[0]
    mixture = jnp.zeros((length, raw_rows.shape[1]), jnp.float32)
    for offset in range(conv_weight.shape[0]):
        mixture = mixture + conv_weight[offset][None, :] * joined[offset : offset + length]
    return jax.nn.silu(mixture).astype(jnp.bfloat16)


def split_conv(conv_out):
    seg_rows = conv_out.shape[0]
    inner_dim = SSM_HEADS * HEAD_DIM
    values = conv_out[:, :inner_dim].reshape(seg_rows, SSM_HEADS, HEAD_DIM)
    inputs_b = conv_out[:, inner_dim : inner_dim + STATE_DIM]
    inputs_c = conv_out[:, inner_dim + STATE_DIM :]
    return (values, inputs_b, inputs_c)


def ssm_local(conv_out, step_rows, decay_rate):
    values, inputs_b, inputs_c = split_conv(conv_out)
    cumulative = jnp.cumsum(-decay_rate[None, :] * step_rows, axis=0)
    total_decay = jnp.exp(cumulative[-1])
    weight_end = jnp.exp(cumulative[-1][None, :] - cumulative) * step_rows
    scaled = (weight_end[:, :, None] * values.astype(jnp.float32)).astype(jnp.bfloat16)
    local_state = jnp.einsum(
        "shp,sn->hpn", scaled, inputs_b, preferred_element_type=jnp.float32
    ).astype(jnp.bfloat16)
    return (local_state, total_decay)


def ssm_output(conv_out, step_rows, decay_rate, skip_gain, initial):
    values, inputs_b, inputs_c = split_conv(conv_out)
    seg_rows = conv_out.shape[0]
    cumulative = jnp.cumsum(-decay_rate[None, :] * step_rows, axis=0)
    scores = jnp.dot(inputs_c, inputs_b.T, preferred_element_type=jnp.float32)
    causal_ordered = jnp.arange(seg_rows)[:, None] >= jnp.arange(seg_rows)[None, :]
    log_gap = cumulative.T[:, :, None] - cumulative.T[:, None, :]
    log_gap = jnp.where(causal_ordered[None], log_gap, -jnp.inf)
    kernel = (scores[None] * jnp.exp(log_gap) * step_rows.T[:, None, :]).astype(jnp.bfloat16)
    intra_out = jnp.einsum("hts,shp->thp", kernel, values, preferred_element_type=jnp.float32)
    carried = jnp.exp(cumulative)[:, :, None] * jnp.einsum(
        "tn,hpn->thp", inputs_c, initial, preferred_element_type=jnp.float32
    )
    summed = intra_out + carried + skip_gain[None, :, None] * values.astype(jnp.float32)
    flat_out = summed.reshape(seg_rows, SSM_HEADS * HEAD_DIM)
    inv_norm = lax.rsqrt(jnp.mean(flat_out * flat_out, axis=-1, keepdims=True) + EPSILON)
    return (flat_out * inv_norm).astype(jnp.bfloat16)


def attend(queries, context, seg_depth):
    seg_rows = queries.shape[0]
    group_size = Q_HEADS // KV_HEADS
    query_vec = queries.reshape(seg_rows, KV_HEADS, group_size, ATT_DIM)
    key_rows = context[:, : KV_HEADS * ATT_DIM].reshape(3 * seg_rows, KV_HEADS, ATT_DIM)
    value_rows = context[:, KV_HEADS * ATT_DIM :].reshape(3 * seg_rows, KV_HEADS, ATT_DIM)
    logits = jnp.einsum(
        "tkgd,jkd->kgtj", query_vec, key_rows, preferred_element_type=jnp.float32
    ) * ATT_DIM ** (-0.5)
    query_pos = jnp.arange(seg_rows)[:, None]
    key_pos = jnp.arange(3 * seg_rows)[None, :] - 2 * seg_rows
    lowest = -seg_rows * seg_depth
    allowed = (key_pos <= query_pos) & (query_pos - key_pos < WINDOW) & (key_pos >= lowest)
    logits = jnp.where(allowed[None, None], logits, -jnp.inf)
    row_peak = jnp.max(logits, axis=-1, keepdims=True)
    weights_raw = jnp.exp(logits - row_peak)
    softmax_w = (weights_raw / jnp.sum(weights_raw, axis=-1, keepdims=True)).astype(jnp.bfloat16)
    attended = jnp.einsum(
        "kgtj,jkd->tkgd", softmax_w, value_rows, preferred_element_type=jnp.float32
    )
    return attended.reshape(seg_rows, Q_HEADS * ATT_DIM).astype(jnp.bfloat16)


def on_device(
    xbc, step_size, queries, keys_values, parent_slot, decay_rate, skip_gain, conv_weight
):
    device_count = lax.axis_size("branch")
    my_slot = lax.axis_index("branch")
    grands = jnp.take(parent_slot, parent_slot)
    my_parent = parent_slot[my_slot]
    my_grand = grands[my_slot]
    is_root = my_parent == my_slot
    seg_depth = jnp.where(is_root, 0, jnp.where(my_grand == my_parent, 1, 2))
    seg_rows = xbc.shape[0]
    tail_len = conv_weight.shape[0] - 1
    pair_block = to_rows(keys_values.reshape(-1), device_count)
    tail_block = to_rows(xbc[seg_rows - tail_len :].reshape(-1), device_count)
    held_pairs, held_tails = (
        lax.all_to_all(pair_block, "branch", split_axis=0, concat_axis=0, tiled=True),
        lax.all_to_all(tail_block, "branch", split_axis=0, concat_axis=0, tiled=True),
    )
    picked = (
        jnp.take(held_pairs, parent_slot, axis=0),
        jnp.take(held_pairs, grands, axis=0),
        jnp.take(held_tails, parent_slot, axis=0),
    )
    pairs_parent, pairs_grand, tail_parent = (
        lax.all_to_all(picked[0], "branch", split_axis=0, concat_axis=0, tiled=True),
        lax.all_to_all(picked[1], "branch", split_axis=0, concat_axis=0, tiled=True),
        lax.all_to_all(picked[2], "branch", split_axis=0, concat_axis=0, tiled=True),
    )
    parent_keys = from_rows(pairs_parent, keys_values.shape)
    grand_keys = from_rows(pairs_grand, keys_values.shape)
    tail_rows = from_rows(tail_parent, (tail_len, xbc.shape[1]))
    tail_rows = jnp.where(is_root, jnp.zeros_like(tail_rows), tail_rows)
    conv_out = forward_only_filter(xbc, tail_rows, conv_weight)
    local_state, total_decay = ssm_local(conv_out, step_size, decay_rate)
    context = jnp.concatenate([grand_keys, parent_keys, keys_values], axis=0)
    attended = attend(queries, context, seg_depth)
    state_shape = local_state.shape

    def relay_state(payload):
        held_state = lax.all_to_all(
            to_rows(payload.reshape(-1), device_count),
            "branch",
            split_axis=0,
            concat_axis=0,
            tiled=True,
        )
        returned = lax.all_to_all(
            jnp.take(held_state, parent_slot, axis=0),
            "branch",
            split_axis=0,
            concat_axis=0,
            tiled=True,
        )
        return from_rows(returned, state_shape)

    first_hop = relay_state(local_state)
    combined = (
        local_state.astype(jnp.float32) + total_decay[:, None, None] * first_hop.astype(jnp.float32)
    ).astype(jnp.bfloat16)
    end_state = jnp.where(is_root, local_state, combined)
    initial = relay_state(end_state)
    initial = jnp.where(is_root, jnp.zeros_like(initial), initial)
    ssm_rows = ssm_output(conv_out, step_size, decay_rate, skip_gain, initial)
    return (ssm_rows, attended)


def solution(mesh):
    in_specs = (
        P(("groups", "branch"), None),
        P(("groups", "branch"), None),
        P(("groups", "branch"), None),
        P(("groups", "branch"), None),
        P("groups"),
        P(),
        P(),
        P(),
    )
    out_specs = (P(("groups", "branch"), None), P(("groups", "branch"), None))
    return jax.shard_map(
        on_device, mesh=mesh, in_specs=in_specs, out_specs=out_specs, check_vma=False
    )
```

profile of v0, /device:TPU:13, one launch (start us, length us, event | category | flops | bytes accessed | tf_op | source)
XLA Modules:
  0.0 450.2 jit_solution(1705516916285689351)
XLA Ops:
  3.9 6.6 %all-to-all-start = ((bf16[16,2,792]{2,1,0:T(2,128)(2,1)}), bf16[16,2,792]{2,1,0:T(2,128)(2,1)S(1)}, u32[]{:S(2)}, u32[]{:S(2)}) async-start(bf16[16,2,792]{2,1,0:T(2,128)(2,1)} %reshape.310), calls=%async_computation | async-start | bytes 114688 | tf_op jit(solution)/shard_map/all_to_all | solution.py:114
  17.3 2.1 all_to_all.84
  19.4 3.8 reduce.25
  27.7 6.0 %all-to-all-start.1 = ((bf16[16,2,792]{2,1,0:T(2,128)(2,1)}), bf16[16,2,792]{2,1,0:T(2,128)(2,1)S(1)}, u32[]{:S(2)}, u32[]{:S(2)}) async-start(bf16[16,2,792]{2,1,0:T(2,128)(2,1)} %reshape.312), calls=%async_computation.1 | async-start | bytes 114688 | tf_op jit(solution)/shard_map/all_to_all | solution.py:124
  34.1 3.9 all-to-all-done.1
  38.0 6.4 %all-to-all-start.6 = ((bf16[16,2,8192]{2,1,0:T(2,128)(2,1)}), bf16[16,2,8192]{2,1,0:T(2,128)(2,1)S(1)}, u32[]{:S(2)}, u32[]{:S(2)}) async-start(bf16[16,2,8192]{2,1,0:T(2,128)(2,1)} %reshape.322), calls=%async_computation.6 | async-start | bytes 1048576 | tf_op jit(solution)/shard_map/all_to_all | solution.py:113
  44.9 3.1 maximum_convert_fusion
  48.0 5.2 %multiply_convert_fusion.1 = bf16[256,8448]{1,0:T(8,128)(2,1)S(1)} fusion(f32[259,8448]{1,0:T(8,128)S(1)} %maximum_convert_fusion, f32[8448]{0:T(1024)S(1)} %get-tuple-element.14, f32[8448]{0:T(1024)S(1)} %get-tuple-element.15, f32[8448]{0:T(1024)S(1)} %get-tuple-element.13, f32[8448]{0:T(1024)S(1)} %get-tuple-element.12), kind=kLoop, calls=%fused_computation.25 | loop fusion | flops 25952256 | bytes 39063552 | tf_op jit(solution)/shard_map/convert_element_type | solution.py:32
  53.3 2.0 copy-done.1
  55.2 2.5 slice.87
  57.8 6.4 %copy.46 = bf16[256,8192]{0,1:T(8,128)(2,1)} copy(bf16[256,8192]{1,0:T(8,128)(2,1)} %slice.87) | data formatting | bytes 8388608 | tf_op jit(solution)/shard_map/slice | solution.py:38
  64.1 3.4 fusion.26
  67.6 6.6 %all_to_all.82 = bf16[16,1,65536]{2,1,0:T(2,128)(2,1)} reshape(bf16[64,128,128]{2,1,0:T(8,128)(2,1)S(1)} %fusion.26) | data formatting | bytes 4194304 | tf_op jit(solution)/shard_map/all_to_all | solution.py:137
  74.2 14.3 %reduce.21 = bf16[16,65536]{1,0:T(8,128)(2,1)} reduce(bf16[16,1,65536]{2,1,0:T(2,128)(2,1)} %all_to_all.82, bf16[]{:T(256)} %broadcast.219), dimensions={1}, to_apply=%all_to_all.82.reduce_sub_computation | reduce | bytes 4194306 | tf_op jit(solution)/shard_map/all_to_all | solution.py:137
  88.5 4.0 reshape.314
  92.4 6.1 %all-to-all-start.2 = ((bf16[16,2,32768]{2,1,0:T(2,128)(2,1)}), bf16[16,2,32768]{2,1,0:T(2,128)(2,1)S(1)}, u32[]{:S(2)}, u32[]{:S(2)}) async-start(bf16[16,2,32768]{2,1,0:T(2,128)(2,1)} %reshape.314), calls=%async_computation.2 | async-start | bytes 4194304 | tf_op jit(solution)/shard_map/all_to_all | solution.py:137
  100.3 1.8 copy.101
  104.7 2.2 select_bitcast_fusion.2
  106.9 2.0 reduce.26
  110.0 35.9 %all-to-all-done.2 = bf16[16,2,32768]{2,1,0:T(2,128)(2,1)S(1)} async-done(((bf16[16,2,32768]{2,1,0:T(2,128)(2,1)}), bf16[16,2,32768]{2,1,0:T(2,128)(2,1)S(1)}, u32[]{:S(2)}, u32[]{:S(2)}) %all-to-all-start.2) | async-done | bytes 2097184 | tf_op jit(solution)/shard_map/all_to_all | solution.py:137
  145.9 5.2 %all-to-all-start.7 = ((bf16[16,2,8192]{2,1,0:T(2,128)(2,1)}), bf16[16,2,8192]{2,1,0:T(2,128)(2,1)S(1)}, u32[]{:S(2)}, u32[]{:S(2)}) async-start(bf16[16,2,8192]{2,1,0:T(2,128)(2,1)} %reshape.324), calls=%async_computation.7 | async-start | bytes 1048576 | tf_op jit(solution)/shard_map/all_to_all | solution.py:123
  151.1 6.7 %reshape.315 = bf16[16,1,65536]{2,1,0:T(2,128)(2,1)} reshape(bf16[16,2,32768]{2,1,0:T(2,128)(2,1)S(1)} %all-to-all-done.2) | data formatting | bytes 4194304
  157.9 4.5 copy.100
  162.4 3.3 gather_fusion.2
  165.6 1.9 select_bitcast_fusion.1
  167.5 2.8 reduce.22
  170.3 4.0 reshape.316
  174.3 6.0 %all-to-all-start.3 = ((bf16[16,2,32768]{2,1,0:T(2,128)(2,1)}), bf16[16,2,32768]{2,1,0:T(2,128)(2,1)S(1)}, u32[]{:S(2)}, u32[]{:S(2)}) async-start(bf16[16,2,32768]{2,1,0:T(2,128)(2,1)} %reshape.316), calls=%async_computation.3 | async-start | bytes 4194304 | tf_op jit(solution)/shard_map/all_to_all | solution.py:144
  180.3 2.0 reduce.27
  183.5 44.3 %all-to-all-done.3 = bf16[16,2,32768]{2,1,0:T(2,128)(2,1)S(1)} async-done(((bf16[16,2,32768]{2,1,0:T(2,128)(2,1)}), bf16[16,2,32768]{2,1,0:T(2,128)(2,1)S(1)}, u32[]{:S(2)}, u32[]{:S(2)}) %all-to-all-start.3) | async-done | bytes 2097184 | tf_op jit(solution)/shard_map/all_to_all | solution.py:144
  227.8 5.5 %all-to-all-start.8 = ((bf16[16,2,8192]{2,1,0:T(2,128)(2,1)}), bf16[16,2,8192]{2,1,0:T(2,128)(2,1)}, u32[]{:S(2)}, u32[]{:S(2)}) async-start(bf16[16,2,8192]{2,1,0:T(2,128)(2,1)} %reshape.326), calls=%async_computation.8 | async-start | bytes 1048576 | tf_op jit(solution)/shard_map/all_to_all | solution.py:122
  233.2 6.7 %reshape.317 = bf16[16,1,65536]{2,1,0:T(2,128)(2,1)} reshape(bf16[16,2,32768]{2,1,0:T(2,128)(2,1)S(1)} %all-to-all-done.3) | data formatting | bytes 4194304
  240.0 6.6 %convert_element_type.61 = f32[16,1,65536]{2,1,0:T(1,128)S(1)} convert(bf16[16,1,65536]{2,1,0:T(2,128)(2,1)} %reshape.317) | non-fusion elementwise | flops 1048576 | bytes 6291456 | tf_op jit(solution)/shard_map/convert_element_type | solution.py:155
  246.6 2.3 fusion.22
  249.0 10.0 %all_to_all.83 = bf16[16,1,65536]{2,1,0:T(2,128)(2,1)} reshape(bf16[64,128,128]{2,1,0:T(8,128)(2,1)} %fusion.22) | data formatting | bytes 4194304 | tf_op jit(solution)/shard_map/all_to_all | solution.py:137
  259.0 12.9 %reduce.23 = bf16[16,65536]{1,0:T(8,128)(2,1)S(1)} reduce(bf16[16,1,65536]{2,1,0:T(2,128)(2,1)} %all_to_all.83, bf16[]{:T(256)} %broadcast.219), dimensions={1}, to_apply=%all_to_all.83.reduce_sub_computation | reduce | bytes 4194306 | tf_op jit(solution)/shard_map/all_to_all | solution.py:137
  271.9 2.7 reshape.318
  274.6 6.3 %all-to-all-start.4 = ((bf16[16,2,32768]{2,1,0:T(2,128)(2,1)}), bf16[16,2,32768]{2,1,0:T(2,128)(2,1)S(1)}, u32[]{:S(2)}, u32[]{:S(2)}) async-start(bf16[16,2,32768]{2,1,0:T(2,128)(2,1)} %reshape.318), calls=%async_computation.4 | async-start | bytes 4194304 | tf_op jit(solution)/shard_map/all_to_all | solution.py:137
  282.7 3.4 copy.74
  288.2 2.2 reshape.325
  290.4 3.9 reduce.9
  294.4 2.1 reshape_reshape.4
  296.5 2.2 reshape.327
  298.7 3.9 reduce.10
  307.1 2.3 copy.58
  309.4 18.8 %all-to-all-done.4 = bf16[16,2,32768]{2,1,0:T(2,128)(2,1)S(1)} async-done(((bf16[16,2,32768]{2,1,0:T(2,128)(2,1)}), bf16[16,2,32768]{2,1,0:T(2,128)(2,1)S(1)}, u32[]{:S(2)}, u32[]{:S(2)}) %all-to-all-start.4) | async-done | bytes 2097184 | tf_op jit(solution)/shard_map/all_to_all | solution.py:137
  328.2 6.7 %reshape.319 = bf16[16,1,65536]{2,1,0:T(2,128)(2,1)} reshape(bf16[16,2,32768]{2,1,0:T(2,128)(2,1)S(1)} %all-to-all-done.4) | data formatting | bytes 4194304
  334.9 4.5 copy.99
  339.4 3.3 gather_fusion.3
  342.7 1.9 select_bitcast_fusion
  344.6 2.8 reduce.24
  347.3 4.0 reshape.320
  351.4 5.2 %all-to-all-start.5 = ((bf16[16,2,32768]{2,1,0:T(2,128)(2,1)}), bf16[16,2,32768]{2,1,0:T(2,128)(2,1)S(1)}, u32[]{:S(2)}, u32[]{:S(2)}) async-start(bf16[16,2,32768]{2,1,0:T(2,128)(2,1)} %reshape.320), calls=%async_computation.5 | async-start | bytes 4194304 | tf_op jit(solution)/shard_map/all_to_all | solution.py:144
  356.6 14.0 %fusion.52 = (f32[4,8,256]{2,1,0:T(8,128)S(1)}, f32[4,8,256,768]{2,3,1,0:T(8,128)}) fusion(pred[256,768]{0,1:T(8,128)(4,1)S(1)} %copy-done.7, bf16[768,4,128,1]{0,2,3,1:T(8,128)(2,1)} %bitcast.104, bf16[256,4,8,128]{3,2,1,0:T(8,128)(2,1)} %bitcast.102), kind=kOutput, calls=%fused_computation.105 | convolution fusion | flops 1635779328 | bytes 28278784 | tf_op jit(solution)/shard_map/sub | solution.py:90
  371.7 11.6 %fusion.25 = bf16[4,128,8,256]{3,1,2,0:T(8,128)(2,1)} fusion(bf16[768,4,128,1]{0,2,3,1:T(8,128)(2,1)} %bitcast.105, f32[4,8,256,768]{2,3,1,0:T(8,128)} %get-tuple-element.28, f32[4,8,256]{2,1,0:T(8,128)S(1)} %get-tuple-element.27), kind=kOutput, calls=%fused_computation.50 | convolution fusion | flops 1624244224 | bytes 28082176 | tf_op jit(solution)/shard_map/kgtj,jkd->tkgd/dot_general | solution.py:92
  383.3 4.1 copy.62
  387.4 16.5 %all-to-all-done.5 = bf16[16,2,32768]{2,1,0:T(2,128)(2,1)S(1)} async-done(((bf16[16,2,32768]{2,1,0:T(2,128)(2,1)}), bf16[16,2,32768]{2,1,0:T(2,128)(2,1)S(1)}, u32[]{:S(2)}, u32[]{:S(2)}) %all-to-all-start.5) | async-done | bytes 2097184 | tf_op jit(solution)/shard_map/all_to_all | solution.py:144
  403.9 6.7 %reshape.321 = bf16[16,1,65536]{2,1,0:T(2,128)(2,1)} reshape(bf16[16,2,32768]{2,1,0:T(2,128)(2,1)S(1)} %all-to-all-done.5) | data formatting | bytes 4194304
  410.6 10.7 %fusion.18 = bf16[16,65536]{1,0:T(8,128)(2,1)S(1)} fusion(bf16[16,1,65536]{2,1,0:T(2,128)(2,1)} %reshape.321, pred[]{:T(512)S(6)} %eq.6), kind=kLoop, calls=%fused_computation.40 | loop fusion | flops 1048576 | bytes 4194305 | tf_op jit(solution)/shard_map/jit(_where)/select_n | solution.py:159
  421.3 2.0 select_n.93
  423.2 3.0 fusion.40
  426.3 8.5 %multiply_reduce_fusion = (f32[256]{0:T(256)S(1)}, f32[256,64,128]{0,2,1:T(8,128)}) fusion(bf16[256,64,128]{0,2,1:T(8,128)(2,1)S(1)} %bitcast.100, f32[64]{0:T(128)S(1)} %copy-done.10, f32[256,64,128]{0,2,1:T(8,128)S(1)} %fusion.40, f32[256,64]{0,1:T(8,128)S(1)} %copy-done.9, f32[64,256]{1,0:T(8,128)S(1)} %bitcast.106, ...), kind=kOutput, calls=%fused_computation.31 | convolution fusion | flops 1109393152 | bytes 21497088 | tf_op jit(solution)/shard_map/hts,shp->thp/dot_general | solution.py:65
  434.8 8.9 %copy.53 = f32[256,8192]{1,0:T(8,128)} copy(f32[256,8192]{0,1:T(8,128)} %bitcast.97) | data formatting | bytes 16777216 | tf_op jit(solution)/shard_map/reshape | solution.py:70
  443.7 6.3 %multiply_convert_fusion.3 = bf16[256,8192]{1,0:T(8,128)(2,1)} fusion(f32[256,8192]{1,0:T(8,128)} %copy.53, f32[256]{0:T(256)S(1)} %add_rsqrt_fusion), kind=kLoop, calls=%fused_computation.30 | loop fusion | flops 4194304 | bytes 12583936 | tf_op jit(solution)/shard_map/convert_element_type | solution.py:72
  (76 shorter events, 29.9 us)
Async XLA Ops:
  0.6 23.8 %copy-start = (s32[16]{0:T(128)S(1)}, s32[16]{0:T(128)}, u32[]{:S(2)}) copy-start(s32[16]{0:T(128)} %param.16) | copy-start | bytes 196
  0.6 33.1 %copy-start.8 = (f32[4,8448]{1,0:T(4,128)S(1)}, f32[4,8448]{1,0:T(4,128)}, u32[]{:S(2)}) copy-start(f32[4,8448]{1,0:T(4,128)} %param.19) | copy-start | bytes 405508
  3.9 21.7 %all-to-all-start = ((bf16[16,2,792]{2,1,0:T(2,128)(2,1)}), bf16[16,2,792]{2,1,0:T(2,128)(2,1)S(1)}, u32[]{:S(2)}, u32[]{:S(2)}) async-start(bf16[16,2,792]{2,1,0:T(2,128)(2,1)} %reshape.310), calls=%async_computation | async-start | bytes 114688 | tf_op jit(solution)/shard_map/all_to_all | solution.py:114
  27.7 10.2 %all-to-all-start.1 = ((bf16[16,2,792]{2,1,0:T(2,128)(2,1)}), bf16[16,2,792]{2,1,0:T(2,128)(2,1)S(1)}, u32[]{:S(2)}, u32[]{:S(2)}) async-start(bf16[16,2,792]{2,1,0:T(2,128)(2,1)} %reshape.312), calls=%async_computation.1 | async-start | bytes 114688 | tf_op jit(solution)/shard_map/all_to_all | solution.py:124
  38.0 54.5 %all-to-all-start.6 = ((bf16[16,2,8192]{2,1,0:T(2,128)(2,1)}), bf16[16,2,8192]{2,1,0:T(2,128)(2,1)S(1)}, u32[]{:S(2)}, u32[]{:S(2)}) async-start(bf16[16,2,8192]{2,1,0:T(2,128)(2,1)} %reshape.322), calls=%async_computation.6 | async-start | bytes 1048576 | tf_op jit(solution)/shard_map/all_to_all | solution.py:113
  53.2 2.0 copy-start.1
  67.6 20.9 %copy-start.2 = (bf16[64,128,128]{2,1,0:T(8,128)(2,1)}, bf16[64,128,128]{2,1,0:T(8,128)(2,1)S(1)}, u32[]{:S(2)}) copy-start(bf16[64,128,128]{2,1,0:T(8,128)(2,1)S(1)} %fusion.26) | copy-start | bytes 6291460
  92.4 53.5 %all-to-all-start.2 = ((bf16[16,2,32768]{2,1,0:T(2,128)(2,1)}), bf16[16,2,32768]{2,1,0:T(2,128)(2,1)S(1)}, u32[]{:S(2)}, u32[]{:S(2)}) async-start(bf16[16,2,32768]{2,1,0:T(2,128)(2,1)} %reshape.314), calls=%async_computation.2 | async-start | bytes 4194304 | tf_op jit(solution)/shard_map/all_to_all | solution.py:137
  145.9 28.4 %all-to-all-start.7 = ((bf16[16,2,8192]{2,1,0:T(2,128)(2,1)}), bf16[16,2,8192]{2,1,0:T(2,128)(2,1)S(1)}, u32[]{:S(2)}, u32[]{:S(2)}) async-start(bf16[16,2,8192]{2,1,0:T(2,128)(2,1)} %reshape.324), calls=%async_computation.7 | async-start | bytes 1048576 | tf_op jit(solution)/shard_map/all_to_all | solution.py:123
  174.3 58.9 %copy-start.5 = (bf16[16,2,8192]{2,1,0:T(2,128)(2,1)}, bf16[16,2,8192]{2,1,0:T(2,128)(2,1)S(1)}, u32[]{:S(2)}) copy-start(bf16[16,2,8192]{2,1,0:T(2,128)(2,1)S(1)} %all-to-all-done.7) | copy-start | bytes 1572868
  174.3 53.4 %all-to-all-start.3 = ((bf16[16,2,32768]{2,1,0:T(2,128)(2,1)}), bf16[16,2,32768]{2,1,0:T(2,128)(2,1)S(1)}, u32[]{:S(2)}, u32[]{:S(2)}) async-start(bf16[16,2,32768]{2,1,0:T(2,128)(2,1)} %reshape.316), calls=%async_computation.3 | async-start | bytes 4194304 | tf_op jit(solution)/shard_map/all_to_all | solution.py:144
  227.8 46.9 %all-to-all-start.8 = ((bf16[16,2,8192]{2,1,0:T(2,128)(2,1)}), bf16[16,2,8192]{2,1,0:T(2,128)(2,1)}, u32[]{:S(2)}, u32[]{:S(2)}) async-start(bf16[16,2,8192]{2,1,0:T(2,128)(2,1)} %reshape.326), calls=%async_computation.8 | async-start | bytes 1048576 | tf_op jit(solution)/shard_map/all_to_all | solution.py:122
  240.0 6.7 %copy-start.3 = (bf16[64,128,128]{2,1,0:T(8,128)(2,1)S(1)}, bf16[64,128,128]{2,1,0:T(8,128)(2,1)}, u32[]{:S(2)}) copy-start(bf16[64,128,128]{2,1,0:T(8,128)(2,1)} %copy-done.2) | copy-start | bytes 6291460
  274.6 53.6 %all-to-all-start.4 = ((bf16[16,2,32768]{2,1,0:T(2,128)(2,1)}), bf16[16,2,32768]{2,1,0:T(2,128)(2,1)S(1)}, u32[]{:S(2)}, u32[]{:S(2)}) async-start(bf16[16,2,32768]{2,1,0:T(2,128)(2,1)} %reshape.318), calls=%async_computation.4 | async-start | bytes 4194304 | tf_op jit(solution)/shard_map/all_to_all | solution.py:137
  347.3 9.2 %copy-start.7 = (pred[256,768]{0,1:T(8,128)(4,1)S(1)}, pred[256,768]{0,1:T(8,128)(4,1)}, u32[]{:S(2)}) copy-start(pred[256,768]{0,1:T(8,128)(4,1)} %fusion.37) | copy-start | bytes 589828
  351.4 52.5 %all-to-all-start.5 = ((bf16[16,2,32768]{2,1,0:T(2,128)(2,1)}), bf16[16,2,32768]{2,1,0:T(2,128)(2,1)S(1)}, u32[]{:S(2)}, u32[]{:S(2)}) async-start(bf16[16,2,32768]{2,1,0:T(2,128)(2,1)} %reshape.320), calls=%async_computation.5 | async-start | bytes 4194304 | tf_op jit(solution)/shard_map/all_to_all | solution.py:144
  423.2 3.0 copy-start.4
  423.2 3.0 copy-start.6
  423.2 3.1 copy-start.9
  423.2 3.1 copy-start.10
where the time goes:
time: 458 us; the launch traced here: 450 us
  local copies, waits for them, and re-layouts  137 us (30%)
  waiting for transfers between devices  119 us (26%)
  other arithmetic  96.5 us (21%)
  starting transfers between devices  53.2 us (12%)
  matrix products  41.6 us (9%)
    unnamed x48, local copies, waits for them, and re-layouts  74.6 us
    all_to_all x2, waiting for transfers between devices, relay_state(): lax.all_to_all(jnp.take(held_state, parent_slot, axis=0), 'branch', split...  60.8 us
    all_to_all x2, waiting for transfers between devices, relay_state(): lax.all_to_all(to_rows(payload.reshape(-1), device_count), 'branch', spli...  54.8 us
    all_to_all x2, other arithmetic, relay_state(): lax.all_to_all(to_rows(payload.reshape(-1), device_count), 'branch', spli...  27.2 us
    all_to_all x2, local copies, waits for them, and re-layouts, relay_state(): lax.all_to_all(to_rows(payload.reshape(-1), device_count), 'branch', spli...  16.6 us
    sub x1, matrix products, attend(): weights_raw = jnp.exp(logits - row_peak)  14 us
    all_to_all x2, starting transfers between devices, relay_state(): lax.all_to_all(to_rows(payload.reshape(-1), device_count), 'branch', spli...  12.3 us
    dot_general x1, matrix products, attend(): jnp.einsum('kgtj,jkd->tkgd', softmax_w, value_rows, preferred_element_typ...  11.6 us
  transfers between devices with their start and end apart: 9, of which 5 were waited for; matrix products, arithmetic and copies ran while one was open for 40% of the time, Pallas kernels for 0%

commit v1 on v0

v1 whole, which is shorter than its diff:
```python
import math

import jax
import jax.numpy as jnp
from jax import lax
from jax.experimental import pallas as pl
from jax.experimental.pallas import tpu as pltpu
from jax.sharding import PartitionSpec as P

SSM_HEADS = 64
HEAD_DIM = 128
STATE_DIM = 128
Q_HEADS = 32
KV_HEADS = 4
ATT_DIM = 128
INNER = SSM_HEADS * HEAD_DIM
EPSILON = 1e-05
LOG2E = math.log2(math.e)
FAR = -1e30
HEAD_BLOCK = 8
COLS = HEAD_BLOCK * HEAD_DIM
VMEM_LIMIT = 50 * 1024 * 1024
bf16, f32 = jnp.bfloat16, jnp.float32


def params():
    return pltpu.CompilerParams(vmem_limit_bytes=VMEM_LIMIT)


def cost(flops, moved, transcendentals=0):
    return pl.CostEstimate(flops=flops, bytes_accessed=moved, transcendentals=transcendentals)


def filtered(x_ref, tail_ref, weight_ref, joined):
    rows, cols = x_ref.shape
    joined[0:8, :cols] = tail_ref[...]
    joined[8 : 8 + rows, :cols] = x_ref[...].astype(f32)
    mixture = weight_ref[3:4, :] * joined[8 : 8 + rows, :cols]
    for tap in range(3):
        mixture += weight_ref[tap : tap + 1, :] * joined[5 + tap : 5 + tap + rows, :cols]
    half = 0.5 * mixture
    return half + half * jnp.tanh(half)


def conv_state_kernel(
    x_ref, bc_ref, tail_ref, tail_bc_ref, w_ref, w_bc_ref, end_ref,
    values_ref, bc_out_ref, state_ref, joined, b_t,
):
    @pl.when(pl.program_id(0) == 0)
    def _():
        bc = filtered(bc_ref, tail_bc_ref, w_bc_ref, joined)
        bc_out_ref[...] = bc.astype(bf16)
        b_t[...] = bc[:, :STATE_DIM].T.astype(bf16)

    values = filtered(x_ref, tail_ref, w_ref, joined).astype(bf16)
    values_ref[...] = values
    scaled = jnp.concatenate(
        [
            (
                end_ref[0, :, k : k + 1]
                * values[:, k * HEAD_DIM : (k + 1) * HEAD_DIM].astype(f32)
            ).astype(bf16)
            for k in range(HEAD_BLOCK)
        ],
        axis=1,
    )
    state_ref[...] = jnp.dot(b_t[...], scaled, preferred_element_type=f32).astype(bf16)


def conv_state(xbc, tail, conv_weight, weight_end):
    rows = xbc.shape[0]
    steps = INNER // COLS
    bc_cols = 2 * STATE_DIM
    bc_at = INNER // bc_cols
    return pl.pallas_call(
        conv_state_kernel,
        grid=(steps,),
        in_specs=[
            pl.BlockSpec((rows, COLS), lambda i: (0, i)),
            pl.BlockSpec((rows, bc_cols), lambda i: (0, bc_at)),
            pl.BlockSpec((8, COLS), lambda i: (0, i)),
            pl.BlockSpec((8, bc_cols), lambda i: (0, bc_at)),
            pl.BlockSpec((4, COLS), lambda i: (0, i)),
            pl.BlockSpec((4, bc_cols), lambda i: (0, bc_at)),
            pl.BlockSpec((1, rows, HEAD_BLOCK), lambda i: (i, 0, 0)),
        ],
        out_specs=[
            pl.BlockSpec((rows, COLS), lambda i: (0, i)),
            pl.BlockSpec((rows, bc_cols), lambda i: (0, 0)),
            pl.BlockSpec((STATE_DIM, COLS), lambda i: (0, i)),
        ],
        out_shape=[
            jax.ShapeDtypeStruct((rows, INNER), bf16),
            jax.ShapeDtypeStruct((rows, bc_cols), bf16),
            jax.ShapeDtypeStruct((STATE_DIM, INNER), bf16),
        ],
        scratch_shapes=[
            pltpu.VMEM((rows + 8, COLS), f32),
            pltpu.VMEM((STATE_DIM, rows), bf16),
        ],
        compiler_params=params(),
        cost_estimate=cost(600_000_000, 11_000_000, 2_200_000),
    )(xbc, xbc, tail, tail, conv_weight, conv_weight, weight_end)


def relay_kernel(parents, held_ref, decay_ref, sent_ref):
    slot = pl.program_id(0)
    parent = parents[slot]
    grand = parents[parent]
    local = held_ref[parent].astype(f32)
    above = held_ref[grand].astype(f32)
    decay = jnp.where(grand == parent, 0.0, 1.0) * decay_ref[parent]
    end = local + decay * above
    sent_ref[0] = jnp.where(parent == slot, 0.0, end).astype(bf16)


def relay_select(parents, held, decays):
    count, rows, cols = held.shape
    return pl.pallas_call(
        relay_kernel,
        grid_spec=pltpu.PrefetchScalarGridSpec(
            num_scalar_prefetch=1,
            grid=(count,),
            in_specs=[
                pl.BlockSpec((count, rows, cols), lambda i, p: (0, 0, 0)),
                pl.BlockSpec((count, 1, cols), lambda i, p: (0, 0, 0)),
            ],
            out_specs=pl.BlockSpec((1, rows, cols), lambda i, p: (i, 0, 0)),
        ),
        out_shape=jax.ShapeDtypeStruct(held.shape, bf16),
        compiler_params=params(),
        cost_estimate=cost(4_000_000, 5_000_000),
    )(parents, held, decays)


def pick_kernel(parents, held_ref, sent_ref):
    slot = pl.program_id(0)
    parent = parents[slot]
    grand = parents[parent]
    sent_ref[0, 0] = held_ref[parent]
    sent_ref[0, 1] = held_ref[grand]


def pick_pairs(parents, held):
    count, rows, cols = held.shape
    return pl.pallas_call(
        pick_kernel,
        grid_spec=pltpu.PrefetchScalarGridSpec(
            num_scalar_prefetch=1,
            grid=(count,),
            in_specs=[pl.BlockSpec((count, rows, cols), lambda i, p: (0, 0, 0))],
            out_specs=pl.BlockSpec((1, 2, rows, cols), lambda i, p: (i, 0, 0, 0)),
        ),
        out_shape=jax.ShapeDtypeStruct((count, 2, rows, cols), bf16),
        compiler_params=params(),
        cost_estimate=cost(0, 1_500_000),
    )(parents, held)


NT = (((1,), (1,)), ((), ()))


def attend_kernel(depth_ref, q_ref, ko, vo, kp, vp, kg, vg, out_ref):
    rows = q_ref.shape[0]
    depth = depth_ref[0]
    parent_bias = jnp.where(depth >= 1, 0.0, FAR)
    grand_bias = jnp.where(depth >= 2, 0.0, FAR)
    row = lax.broadcasted_iota(jnp.int32, (rows, rows), 0)
    col = lax.broadcasted_iota(jnp.int32, (rows, rows), 1)
    own_side = col <= row
    rate = ATT_DIM ** (-0.5) * LOG2E
    keys_own, keys_parent, keys_grand = ko[...], kp[...], kg[...]
    values_own, values_parent, values_grand = vo[...], vp[...], vg[...]
    for g in range(q_ref.shape[1] // ATT_DIM):
        at = slice(g * ATT_DIM, (g + 1) * ATT_DIM)
        q = q_ref[:, at]
        own = lax.dot_general(q, keys_own, NT, preferred_element_type=f32)
        grand = lax.dot_general(q, keys_grand, NT, preferred_element_type=f32)
        parent = lax.dot_general(q, keys_parent, NT, preferred_element_type=f32) + parent_bias
        mixed = jnp.where(own_side, own, grand + grand_bias)
        peak = jnp.max(jnp.maximum(mixed, parent), axis=1, keepdims=True)
        mixed = jnp.exp2((mixed - peak) * rate)
        parent = jnp.exp2((parent - peak) * rate)
        total = jnp.sum(mixed + parent, axis=1, keepdims=True)
        own = jnp.where(own_side, mixed, 0.0).astype(bf16)
        grand = jnp.where(own_side, 0.0, mixed).astype(bf16)
        out = jnp.dot(own, values_own, preferred_element_type=f32)
        out += jnp.dot(parent.astype(bf16), values_parent, preferred_element_type=f32)
        out += jnp.dot(grand, values_grand, preferred_element_type=f32)
        out_ref[:, at] = (out * (1.0 / total)).astype(bf16)


def attend(depth, queries, own, parent, grand):
    rows, width = queries.shape
    block = width // KV_HEADS
    key = pl.BlockSpec((rows, ATT_DIM), lambda i, d: (0, i))
    value = pl.BlockSpec((rows, ATT_DIM), lambda i, d: (0, KV_HEADS + i))
    return pl.pallas_call(
        attend_kernel,
        grid_spec=pltpu.PrefetchScalarGridSpec(
            num_scalar_prefetch=1,
            grid=(KV_HEADS,),
            in_specs=[pl.BlockSpec((rows, block), lambda i, d: (0, i))] + [key, value] * 3,
            out_specs=pl.BlockSpec((rows, block), lambda i, d: (0, i)),
        ),
        out_shape=jax.ShapeDtypeStruct(queries.shape, bf16),
        compiler_params=params(),
        cost_estimate=cost(3_300_000_000, 6_000_000, 4_200_000),
    )(depth, queries, own, own, parent, parent, grand, grand)


def intra_kernel(values_ref, bc_ref, cum_ref, gap_ref, gain_ref, out_ref, scores):
    rows = values_ref.shape[0]
    row = lax.broadcasted_iota(jnp.int32, (rows, rows), 0)
    col = lax.broadcasted_iota(jnp.int32, (rows, rows), 1)
    causal = col <= row

    @pl.when(pl.program_id(0) == 0)
    def _():
        scores[...] = lax.dot_general(
            bc_ref[:, STATE_DIM:], bc_ref[:, :STATE_DIM], NT, preferred_element_type=f32
        )

    for k in range(HEAD_BLOCK):
        at = slice(k * HEAD_DIM, (k + 1) * HEAD_DIM)
        power = jnp.where(causal, cum_ref[0, :, k : k + 1] - gap_ref[k : k + 1, :], FAR)
        kernel = (scores[...] * jnp.exp2(power)).astype(bf16)
        values = values_ref[:, at]
        out = jnp.dot(kernel, values, preferred_element_type=f32)
        out_ref[:, at] = out + gain_ref[:, at] * values.astype(f32)


def intra(values, bc, cum2, gap2, gain):
    rows = values.shape[0]
    wide = pl.BlockSpec((rows, COLS), lambda i: (0, i))
    return pl.pallas_call(
        intra_kernel,
        grid=(INNER // COLS,),
        in_specs=[
            wide,
            pl.BlockSpec((rows, 2 * STATE_DIM), lambda i: (0, 0)),
            pl.BlockSpec((1, rows, HEAD_BLOCK), lambda i: (i, 0, 0)),
            pl.BlockSpec((HEAD_BLOCK, rows), lambda i: (i, 0)),
            pl.BlockSpec((1, COLS), lambda i: (0, i)),
        ],
        out_specs=wide,
        out_shape=jax.ShapeDtypeStruct((rows, INNER), f32),
        scratch_shapes=[pltpu.VMEM((rows, rows), f32)],
        compiler_params=params(),
        cost_estimate=cost(1_100_000_000, 12_600_000, 4_200_000),
    )(values, bc, cum2, gap2, gain)


def finish_kernel(intra_ref, c_ref, initial_ref, grow_ref, out_ref, summed, squares):
    step = pl.program_id(0)
    last = pl.num_programs(0) - 1
    carried = jnp.dot(c_ref[...], initial_ref[...], preferred_element_type=f32)
    mixer = intra_ref[...] + jnp.concatenate(
        [
            grow_ref[0, :, k : k + 1] * carried[:, k * HEAD_DIM : (k + 1) * HEAD_DIM]
            for k in range(HEAD_BLOCK)
        ],
        axis=1,
    )
    square = mixer * mixer
    part = square[:, :HEAD_DIM]
    for k in range(1, HEAD_BLOCK):
        part += square[:, k * HEAD_DIM : (k + 1) * HEAD_DIM]
    summed[step] = mixer
    squares[...] = jnp.where(step == 0, part, squares[...] + part)

    @pl.when(step == last)
    def _():
        mean = jnp.sum(squares[...], axis=1, keepdims=True) * (1.0 / INNER)
        scale = lax.rsqrt(mean + EPSILON)
        for s in range(INNER // COLS):
            out_ref[:, s * COLS : (s + 1) * COLS] = (summed[s] * scale).astype(bf16)


def finish(intra_rows, bc, initial, grow):
    rows = intra_rows.shape[0]
    steps = INNER // COLS
    return pl.pallas_call(
        finish_kernel,
        grid=(steps,),
        in_specs=[
            pl.BlockSpec((rows, COLS), lambda i: (0, i)),
            pl.BlockSpec((rows, STATE_DIM), lambda i: (0, 1)),
            pl.BlockSpec((STATE_DIM, COLS), lambda i: (0, i)),
            pl.BlockSpec((1, rows, HEAD_BLOCK), lambda i: (i, 0, 0)),
        ],
        out_specs=pl.BlockSpec((rows, INNER), lambda i: (0, 0)),
        out_shape=jax.ShapeDtypeStruct((rows, INNER), bf16),
        scratch_shapes=[
            pltpu.VMEM((steps, rows, COLS), f32),
            pltpu.VMEM((rows, HEAD_DIM), f32),
        ],
        compiler_params=params(),
        cost_estimate=cost(600_000_000, 14_600_000),
    )(intra_rows, bc, initial, grow)


def prefix_sum(terms):
    rows = terms.shape[0]
    lower = (jnp.arange(rows)[:, None] >= jnp.arange(rows)[None, :]).astype(f32)
    return jnp.dot(lower, terms, precision=lax.Precision.HIGHEST, preferred_element_type=f32)


def by_block(columns):
    rows, heads = columns.shape
    return columns.reshape(rows, heads // HEAD_BLOCK, HEAD_BLOCK).transpose(1, 0, 2)


def exchange(rows):
    return lax.all_to_all(rows, "branch", split_axis=0, concat_axis=0, tiled=True)


def on_device(
    xbc, step_size, queries, keys_values, parent_slot, decay_rate, skip_gain, conv_weight
):
    count = lax.axis_size("branch")
    me = lax.axis_index("branch")
    rows = xbc.shape[0]
    taps = conv_weight.shape[0] - 1
    my_parent = parent_slot[me]
    my_grand = parent_slot[my_parent]
    is_root = my_parent == me
    depth = jnp.where(is_root, 0, jnp.where(my_grand == my_parent, 1, 2)).astype(jnp.int32)

    tails = lax.all_gather(xbc[rows - taps :], "branch")
    held_pairs = exchange(keys_values.reshape(count, rows // count, -1))

    cumulative = prefix_sum(-decay_rate[None, :] * step_size)
    last = cumulative[-1:]
    weight_end = by_block(jnp.exp(last - cumulative) * step_size)
    decays = lax.all_gather(jnp.exp(last), "branch")
    decays = jnp.broadcast_to(decays[:, :, :, None], (count, 1, SSM_HEADS, HEAD_DIM))
    decays = decays.reshape(count, 1, INNER)
    grow = by_block(jnp.exp(cumulative))
    cum2 = by_block(cumulative * LOG2E)
    gap2 = ((cumulative - jnp.log(step_size)) * LOG2E).T
    gain = jnp.broadcast_to(skip_gain[:, None], (SSM_HEADS, HEAD_DIM)).reshape(1, INNER)

    tail = lax.dynamic_index_in_dim(tails, my_parent, 0, keepdims=False).astype(f32)
    tail = jnp.where(is_root, 0.0, tail)
    tail = jnp.concatenate([jnp.zeros((8 - taps, tail.shape[1]), f32), tail], axis=0)
    values, bc, state = conv_state(xbc, tail, conv_weight, weight_end)

    held = exchange(state.reshape(count, STATE_DIM // count, INNER))
    initial = exchange(relay_select(parent_slot, held, decays)).reshape(STATE_DIM, INNER)

    pairs = exchange(pick_pairs(parent_slot, held_pairs))
    parent_pairs = pairs[:, 0].reshape(rows, -1)
    grand_pairs = pairs[:, 1].reshape(rows, -1)
    attended = attend(depth[None], queries, keys_values, parent_pairs, grand_pairs)
    intra_rows = intra(values, bc, cum2, gap2, gain)
    return (finish(intra_rows, bc, initial, grow), attended)


def solution(mesh):
    rows = P(("groups", "branch"), None)
    in_specs = (rows, rows, rows, rows, P("groups"), P(), P(), P())
    return jax.shard_map(
        on_device, mesh=mesh, in_specs=in_specs, out_specs=(rows, rows), check_vma=False
    )
```

time: 458 us -> 209 us (0.46); the launches traced: 450 us -> 208 us
  local copies, waits for them, and re-layouts: 137 us -> 8.68 us
  other arithmetic: 96.5 us -> 0.13 us
  waiting for transfers between devices: 119 us -> 60.8 us
  blocking collectives: 0 us -> 56.7 us
  Pallas kernels: 0 us -> 53.8 us
  matrix products: 41.6 us -> 0.28 us
  starting transfers between devices: 53.2 us -> 23.2 us
    unnamed x48 -> x23, local copies, waits for them, and re-layouts: 74.6 us -> 4.24 us
    all_to_all x9 -> x4, waiting for transfers between devices: 119 us -> 60.8 us  [exchange(): lax.all_to_all(rows, 'branch', split_axis=0, concat_axis=0, tiled=True)]
    all_gather x0 -> x2, blocking collectives: none -> 56.7 us  [the longest x1 34.3 us: on_device(): decays = lax.all_gather(jnp.exp(last), 'branch')]
    all_to_all x13 -> x0, other arithmetic: 55.1 us -> none  [the longest x2 27.2 us: relay_state(): lax.all_to_all(to_rows(payload.reshape(-1), device_count), 'branch', spli...]
    pallas_call x0 -> x6, Pallas kernels: none -> 53.8 us  [the longest x1 14.2 us: attend(): pl.pallas_call(attend_kernel, grid_spec=pltpu.PrefetchScalarGridSpec(num_...]
    all_to_all x9 -> x4, starting transfers between devices: 53.2 us -> 23.2 us  [exchange(): lax.all_to_all(rows, 'branch', split_axis=0, concat_axis=0, tiled=True)]
    dot_general x5 -> x1, matrix products: 27.6 us -> 0.28 us  [prefix_sum(): jnp.dot(lower, terms, precision=lax.Precision.HIGHEST, preferred_element_...]
    convert_element_type x4 -> x0, other arithmetic: 21.3 us -> none  [the longest x1 6.65 us: on_device(): first_hop.astype(jnp.float32)]
  transfers between devices with their start and end apart: 9 -> 4, of which waited for: 5 -> 2; matrix products, arithmetic and copies ran while one was open for 40% -> 3% of each run, Pallas kernels for 0% -> 21%
where the time goes in v1:
time: 209 us; the launch traced here: 208 us
  waiting for transfers between devices  60.8 us (29%)
  blocking collectives  56.7 us (27%)
  Pallas kernels  53.8 us (26%)
  starting transfers between devices  23.2 us (11%)
  local copies, waits for them, and re-layouts  8.68 us (4%)
  between operations  4.82 us (2%)
    all_to_all x4, waiting for transfers between devices, exchange(): lax.all_to_all(rows, 'branch', split_axis=0, concat_axis=0, tiled=True)  60.8 us
    all_gather x1, blocking collectives, on_device(): decays = lax.all_gather(jnp.exp(last), 'branch')  34.3 us
    all_to_all x4, starting transfers between devices, exchange(): lax.all_to_all(rows, 'branch', split_axis=0, concat_axis=0, tiled=True)  23.2 us
    all_gather x1, blocking collectives, on_device(): tails = lax.all_gather(xbc[rows - taps:], 'branch')  22.5 us
    pallas_call x1, Pallas kernels, attend(): pl.pallas_call(attend_kernel, grid_spec=pltpu.PrefetchScalarGridSpec(num_...  14.2 us
    pallas_call x1, Pallas kernels, conv_state(): pl.pallas_call(conv_state_kernel, grid=(steps,), in_specs=[pl.BlockSpec((...  10.7 us
    pallas_call x1, Pallas kernels, finish(): pl.pallas_call(finish_kernel, grid=(steps,), in_specs=[pl.BlockSpec((rows...  10.2 us
    pallas_call x1, Pallas kernels, intra(): pl.pallas_call(intra_kernel, grid=(INNER // COLS,), in_specs=[wide, pl.Bl...  9.74 us
  transfers between devices with their start and end apart: 4, of which 2 were waited for; matrix products, arithmetic and copies ran while one was open for 3% of the time, Pallas kernels for 21%

profile of v1, /device:TPU:13, one launch (start us, length us, event | category | flops | bytes accessed | tf_op | source)
XLA Modules:
  0.0 208.4 jit_solution(2639244018629133589)
XLA Ops:
  0.6 0.0 copy-start.10
  0.6 0.0 copy-start.8
  0.7 0.0 copy-start.2
  0.7 6.7 %all-to-all-start.2 = ((bf16[16,16,1024]{2,1,0:T(8,128)(2,1)}), bf16[16,16,1024]{2,1,0:T(8,128)(2,1)S(1)}, u32[]{:S(2)}, u32[]{:S(2)}) async-start(bf16[16,16,1024]{2,1,0:T(8,128)(2,1)} %bitcast.32), calls=%async_computation.2 | async-start | bytes 1048576 | tf_op jit(solution)/shard_map/all_to_all | solution.py:315
  7.4 1.3 dynamic_slice.10
  10.8 0.9 slice_bitcast_fusion
  11.7 22.5 %all-gather.2 = bf16[16,3,8448]{2,1,0:T(4,128)(2,1)S(1)} all-gather(bf16[1,3,8448]{2,1,0:T(4,128)(2,1)S(1)} %slice_bitcast_fusion), channel_id=2, replica_groups=mesh['groups'=2,'branch'=16] {'branch'}, dimensions={0}, use_global_device_ids=true | all-gather | bytes 861696 | tf_op jit(solution)/shard_map/all_gather | solution.py:330
  34.2 0.0 copy-done.10
  34.2 0.0 copy-done.8
  34.2 0.3 fusion
  34.5 0.2 exponential_reduce_fusion
  34.7 0.1 multiply_bitcast_fusion
  34.8 0.3 copy.14
  35.9 0.0 copy-done.2
  35.9 10.7 %shard_map.95 = (bf16[256,8192]{1,0:T(8,128)(2,1)}, bf16[256,256]{1,0:T(8,128)(2,1)S(1)}, bf16[128,8192]{1,0:T(8,128)(2,1)}) custom-call(bf16[256,8448]{1,0:T(8,128)(2,1)} %bc_ref.1, bf16[256,8448]{1,0:T(8,128)(2,1)} %bc_ref.1, f32[8,8448]{1,0:T(8,128)S(1)} %concatenate.3.tail_ref.tail_bc_ref, f32[8,8448]{1,0:T(8,128)S(1)} %concatenate.3.tail_ref.tail_bc_ref, ...), custom_call_target="tpu_custom_call" | custom-call | flops 600000000 | bytes 11000000 | tf_op jit(solution)/shard_map/pallas_call | solution.py:75
  46.6 0.0 all-to-all-done.2.held_ref
  46.6 0.0 copy-start.4
  46.6 6.6 %all-to-all-start = ((bf16[16,8,8192]{2,1,0:T(8,128)(2,1)}), bf16[16,8,8192]{2,1,0:T(8,128)(2,1)}, u32[]{:S(2)}, u32[]{:S(2)}) async-start(bf16[16,8,8192]{2,1,0:T(8,128)(2,1)} %bitcast.9), calls=%async_computation | async-start | bytes 4194304 | tf_op jit(solution)/shard_map/all_to_all | solution.py:315
  53.3 0.0 copy-done.4
  53.3 5.6 %shard_map.99 = bf16[16,2,16,1024]{3,2,1,0:T(8,128)(2,1)} custom-call(s32[16]{0:T(128)S(1)} %copy-done.4, bf16[16,16,1024]{2,1,0:T(8,128)(2,1)S(1)} %all-to-all-done.2.held_ref), custom_call_target="tpu_custom_call" | custom-call | bytes 1500000 | tf_op jit(solution)/shard_map/pallas_call | solution.py:146
  58.9 41.9 %all-to-all-done.held_ref = bf16[16,8,8192]{2,1,0:T(8,128)(2,1)} async-done(((bf16[16,8,8192]{2,1,0:T(8,128)(2,1)}), bf16[16,8,8192]{2,1,0:T(8,128)(2,1)}, u32[]{:S(2)}, u32[]{:S(2)}) %all-to-all-start) | async-done | bytes 2097184 | tf_op jit(solution)/shard_map/all_to_all | solution.py:315
  100.8 4.9 %all-to-all-start.3 = ((bf16[16,2,16,1024]{3,2,1,0:T(8,128)(2,1)}), bf16[16,2,16,1024]{3,2,1,0:T(8,128)(2,1)S(1)}, u32[]{:S(2)}, u32[]{:S(2)}) async-start(bf16[16,2,16,1024]{3,2,1,0:T(8,128)(2,1)} %shard_map.99), calls=%async_computation.3 | async-start | bytes 2097152 | tf_op jit(solution)/shard_map/all_to_all | solution.py:315
  105.7 34.3 %all-gather.3 = f32[16,1,64]{2,1,0:T(1,128)S(1)} all-gather(f32[1,1,64]{2,1,0:T(1,128)S(1)} %bitcast.39), channel_id=3, replica_groups=mesh['groups'=2,'branch'=16] {'branch'}, dimensions={0}, use_global_device_ids=true | all-gather | bytes 4352 | tf_op jit(solution)/shard_map/all_gather | solution.py:336
  139.9 0.2 broadcast_in_dim.30
  140.1 3.4 %shard_map.97 = bf16[16,8,8192]{2,1,0:T(8,128)(2,1)S(1)} custom-call(s32[16]{0:T(128)S(1)} %copy-done.4, bf16[16,8,8192]{2,1,0:T(8,128)(2,1)} %all-to-all-done.held_ref, f32[16,1,8192]{2,1,0:T(1,128)S(1)} %bitcast.31), custom_call_target="tpu_custom_call" | custom-call | flops 4000000 | bytes 5000000 | tf_op jit(solution)/shard_map/pallas_call | solution.py:119
  143.5 0.0 copy-start
  143.5 1.4 copy-done
  144.9 0.0 all-to-all-done.3
  144.9 0.0 copy-start.6
  144.9 1.0 copy-done.6
  145.9 5.0 %all-to-all-start.1 = ((bf16[16,8,8192]{2,1,0:T(8,128)(2,1)}), bf16[16,8,8192]{2,1,0:T(8,128)(2,1)S(1)}, u32[]{:S(2)}, u32[]{:S(2)}) async-start(bf16[16,8,8192]{2,1,0:T(8,128)(2,1)} %copy-done), calls=%async_computation.1 | async-start | bytes 4194304 | tf_op jit(solution)/shard_map/all_to_all | solution.py:315
  150.8 0.0 copy-start.9
  150.8 0.6 dynamic_slice.12
  151.4 0.3 copy.15
  151.7 1.3 copy.16
  154.3 0.0 copy-done.9
  154.3 0.1 broadcast_in_dim.28
  154.4 0.0 copy-start.7
  154.4 0.0 copy-start.5
  154.4 9.7 %shard_map.96.intra_ref = f32[256,8192]{1,0:T(8,128)} custom-call(bf16[256,8192]{1,0:T(8,128)(2,1)} %get-tuple-element.5.values_ref, bf16[256,256]{1,0:T(8,128)(2,1)S(1)} %get-tuple-element.6.bc_ref.c_ref, f32[8,256,8]{2,1,0:T(8,128)S(1)} %bitcast.29, f32[64,256]{1,0:T(8,128)S(1)} %get-tuple-element.12.gap_ref, f32[1,8192]{1,0:T(1,128)S(1)} %bitcast.37), custom_call_target="tpu_custom_call" | custom-call | flops 1100000000 | bytes 12600000 | tf_op jit(solution)/shard_map/pallas_call | solution.py:236
  164.1 0.0 copy-done.7
  164.1 0.0 copy-start.3
  164.1 0.1 fusion.3
  164.3 0.0 copy-done.5
  164.3 0.9 copy-done.3
  165.2 0.0 copy-start.1
  165.2 14.2 %shard_map.100 = bf16[256,4096]{1,0:T(8,128)(2,1)} custom-call(s32[1]{0:T(128)} %bitcast.16.depth_ref, bf16[256,4096]{1,0:T(8,128)(2,1)S(1)} %copy-done.5, bf16[256,1024]{1,0:T(8,128)(2,1)S(1)} %copy-done.3, bf16[256,1024]{1,0:T(8,128)(2,1)S(1)} %copy-done.3, bf16[256,1024]{1,0:T(8,128)(2,1)S(1)} %bitcast.35, bf16[256,1024]{1,0:T(8,128)(2,1)S(1)} %bitcast.36, ...), custom_call_target="tpu_custom_call" | custom-call | flops 3300000000 | bytes 6000000 | tf_op jit(solution)/shard_map/pallas_call | solution.py:198
  179.4 18.8 %all-to-all-done.1 = bf16[16,8,8192]{2,1,0:T(8,128)(2,1)S(1)} async-done(((bf16[16,8,8192]{2,1,0:T(8,128)(2,1)}), bf16[16,8,8192]{2,1,0:T(8,128)(2,1)S(1)}, u32[]{:S(2)}, u32[]{:S(2)}) %all-to-all-start.1) | async-done | bytes 2097184 | tf_op jit(solution)/shard_map/all_to_all | solution.py:315
  198.3 0.0 copy-done.1
  198.3 10.2 %shard_map.98 = bf16[256,8192]{1,0:T(8,128)(2,1)} custom-call(f32[256,8192]{1,0:T(8,128)} %shard_map.96.intra_ref, bf16[256,256]{1,0:T(8,128)(2,1)S(1)} %get-tuple-element.6.bc_ref.c_ref, bf16[128,8192]{1,0:T(8,128)(2,1)S(1)} %bitcast.27, f32[8,256,8]{2,1,0:T(8,128)S(1)} %bitcast.30), custom_call_target="tpu_custom_call" | custom-call | flops 600000000 | bytes 14600000 | tf_op jit(solution)/shard_map/pallas_call | solution.py:283
  (3 shorter events, 0.1 us)
Async XLA Ops:
  0.6 33.5 %copy-start.10 = (f32[64]{0:T(128)S(1)}, f32[64]{0:T(128)}, u32[]{:S(2)}) copy-start(f32[64]{0:T(128)} %param.13) | copy-start | bytes 772
  0.6 33.5 %copy-start.8 = (f32[256,64]{0,1:T(8,128)S(1)}, f32[256,64]{0,1:T(8,128)}, u32[]{:S(2)}) copy-start(f32[256,64]{0,1:T(8,128)} %param.9) | copy-start | bytes 196612
  0.7 35.2 %copy-start.2 = (f32[4,8448]{1,0:T(4,128)S(1)}, f32[4,8448]{1,0:T(4,128)}, u32[]{:S(2)}) copy-start(f32[4,8448]{1,0:T(4,128)} %w_bc_ref.1) | copy-start | bytes 405508
  0.7 45.9 %all-to-all-start.2 = ((bf16[16,16,1024]{2,1,0:T(8,128)(2,1)}), bf16[16,16,1024]{2,1,0:T(8,128)(2,1)S(1)}, u32[]{:S(2)}, u32[]{:S(2)}) async-start(bf16[16,16,1024]{2,1,0:T(8,128)(2,1)} %bitcast.32), calls=%async_computation.2 | async-start | bytes 1048576 | tf_op jit(solution)/shard_map/all_to_all | solution.py:315
  46.6 6.7 %copy-start.4 = (s32[16]{0:T(128)S(1)}, s32[16]{0:T(128)}, u32[]{:S(2)}) copy-start(s32[16]{0:T(128)} %parents.3) | copy-start | bytes 196
  46.6 54.2 %all-to-all-start = ((bf16[16,8,8192]{2,1,0:T(8,128)(2,1)}), bf16[16,8,8192]{2,1,0:T(8,128)(2,1)}, u32[]{:S(2)}, u32[]{:S(2)}) async-start(bf16[16,8,8192]{2,1,0:T(8,128)(2,1)} %bitcast.9), calls=%async_computation | async-start | bytes 4194304 | tf_op jit(solution)/shard_map/all_to_all | solution.py:315
  100.8 44.1 %all-to-all-start.3 = ((bf16[16,2,16,1024]{3,2,1,0:T(8,128)(2,1)}), bf16[16,2,16,1024]{3,2,1,0:T(8,128)(2,1)S(1)}, u32[]{:S(2)}, u32[]{:S(2)}) async-start(bf16[16,2,16,1024]{3,2,1,0:T(8,128)(2,1)} %shard_map.99), calls=%async_computation.3 | async-start | bytes 2097152 | tf_op jit(solution)/shard_map/all_to_all | solution.py:315
  143.5 1.4 copy-start
  144.9 1.0 copy-start.6
  145.9 52.4 %all-to-all-start.1 = ((bf16[16,8,8192]{2,1,0:T(8,128)(2,1)}), bf16[16,8,8192]{2,1,0:T(8,128)(2,1)S(1)}, u32[]{:S(2)}, u32[]{:S(2)}) async-start(bf16[16,8,8192]{2,1,0:T(8,128)(2,1)} %copy-done), calls=%async_computation.1 | async-start | bytes 4194304 | tf_op jit(solution)/shard_map/all_to_all | solution.py:315
  150.8 3.5 %copy-start.9 = (f32[64]{0:T(128)S(1)}, f32[64]{0:T(128)}, u32[]{:S(2)}) copy-start(f32[64]{0:T(128)} %param.14) | copy-start | bytes 772
  154.4 9.8 %copy-start.7 = (bf16[16,2,16,1024]{3,2,1,0:T(8,128)(2,1)S(1)}, bf16[16,2,16,1024]{3,2,1,0:T(8,128)(2,1)}, u32[]{:S(2)}) copy-start(bf16[16,2,16,1024]{3,2,1,0:T(8,128)(2,1)} %copy-done.6) | copy-start | bytes 3145732
  154.4 9.9 %copy-start.5 = (bf16[256,4096]{1,0:T(8,128)(2,1)S(1)}, bf16[256,4096]{1,0:T(8,128)(2,1)}, u32[]{:S(2)}) copy-start(bf16[256,4096]{1,0:T(8,128)(2,1)} %q_ref.1) | copy-start | bytes 6291460
  164.1 1.0 copy-start.3
  165.2 33.1 %copy-start.1 = (f32[256,8,8]{2,0,1:T(8,128)S(1)}, f32[256,8,8]{2,0,1:T(8,128)}, u32[]{:S(2)}) copy-start(f32[256,8,8]{2,0,1:T(8,128)} %copy.16) | copy-start | bytes 196612

commit v2 on v1

--- a/solution.py
+++ b/solution.py
@@ -133,36 +133,12 @@
     )(parents, held, decays)
 
 
-def pick_kernel(parents, held_ref, sent_ref):
-    slot = pl.program_id(0)
-    parent = parents[slot]
-    grand = parents[parent]
-    sent_ref[0, 0] = held_ref[parent]
-    sent_ref[0, 1] = held_ref[grand]
-
-
-def pick_pairs(parents, held):
-    count, rows, cols = held.shape
-    return pl.pallas_call(
-        pick_kernel,
-        grid_spec=pltpu.PrefetchScalarGridSpec(
-            num_scalar_prefetch=1,
-            grid=(count,),
-            in_specs=[pl.BlockSpec((count, rows, cols), lambda i, p: (0, 0, 0))],
-            out_specs=pl.BlockSpec((1, 2, rows, cols), lambda i, p: (i, 0, 0, 0)),
-        ),
-        out_shape=jax.ShapeDtypeStruct((count, 2, rows, cols), bf16),
-        compiler_params=params(),
-        cost_estimate=cost(0, 1_500_000),
-    )(parents, held)
-
-
 NT = (((1,), (1,)), ((), ()))
 
 
-def attend_kernel(depth_ref, q_ref, ko, vo, kp, vp, kg, vg, out_ref):
+def attend_kernel(lineage, q_ref, ko, vo, kp, vp, kg, vg, out_ref):
     rows = q_ref.shape[0]
-    depth = depth_ref[0]
+    depth = lineage[0]
     parent_bias = jnp.where(depth >= 1, 0.0, FAR)
     grand_bias = jnp.where(depth >= 2, 0.0, FAR)
     row = lax.broadcasted_iota(jnp.int32, (rows, rows), 0)
@@ -190,23 +166,32 @@
         out_ref[:, at] = (out * (1.0 / total)).astype(bf16)
 
 
-def attend(depth, queries, own, parent, grand):
+def attend(lineage, queries, own, gathered):
     rows, width = queries.shape
     block = width // KV_HEADS
-    key = pl.BlockSpec((rows, ATT_DIM), lambda i, d: (0, i))
-    value = pl.BlockSpec((rows, ATT_DIM), lambda i, d: (0, KV_HEADS + i))
+
+    def of(place):
+        return [
+            pl.BlockSpec((None, rows, ATT_DIM), lambda i, d: (d[place], 0, i)),
+            pl.BlockSpec((None, rows, ATT_DIM), lambda i, d: (d[place], 0, KV_HEADS + i)),
+        ]
+
+    mine = [
+        pl.BlockSpec((rows, ATT_DIM), lambda i, d: (0, i)),
+        pl.BlockSpec((rows, ATT_DIM), lambda i, d: (0, KV_HEADS + i)),
+    ]
     return pl.pallas_call(
         attend_kernel,
         grid_spec=pltpu.PrefetchScalarGridSpec(
             num_scalar_prefetch=1,
             grid=(KV_HEADS,),
-            in_specs=[pl.BlockSpec((rows, block), lambda i, d: (0, i))] + [key, value] * 3,
+            in_specs=[pl.BlockSpec((rows, block), lambda i, d: (0, i))] + mine + of(1) + of(2),
             out_specs=pl.BlockSpec((rows, block), lambda i, d: (0, i)),
         ),
         out_shape=jax.ShapeDtypeStruct(queries.shape, bf16),
         compiler_params=params(),
         cost_estimate=cost(3_300_000_000, 6_000_000, 4_200_000),
-    )(depth, queries, own, own, parent, parent, grand, grand)
+    )(lineage, queries, own, own, *[gathered] * 4)
 
 
 def intra_kernel(values_ref, bc_ref, cum_ref, gap_ref, gain_ref, out_ref, scores):
@@ -327,13 +312,19 @@
     is_root = my_parent == me
     depth = jnp.where(is_root, 0, jnp.where(my_grand == my_parent, 1, 2)).astype(jnp.int32)
 
-    tails = lax.all_gather(xbc[rows - taps :], "branch")
-    held_pairs = exchange(keys_values.reshape(count, rows // count, -1))
-
     cumulative = prefix_sum(-decay_rate[None, :] * step_size)
     last = cumulative[-1:]
     weight_end = by_block(jnp.exp(last - cumulative) * step_size)
-    decays = lax.all_gather(jnp.exp(last), "branch")
+    fall = jnp.exp(-decay_rate * jnp.sum(step_size, axis=0))
+    high = lax.reduce_precision(fall, 8, 7)
+    parts = jnp.concatenate([high, fall - high]).astype(bf16)
+    extra = jnp.pad(parts, (0, xbc.shape[1] - parts.shape[0]))[None]
+    gathered = lax.all_gather(jnp.concatenate([xbc[rows - taps :], extra]), "branch")
+    gathered, shared_pairs = lax.optimization_barrier((gathered, keys_values))
+    all_pairs = lax.all_gather(shared_pairs, "branch")
+    tails = gathered[:, :taps]
+    decays = gathered[:, taps:, :SSM_HEADS].astype(f32)
+    decays += gathered[:, taps:, SSM_HEADS : 2 * SSM_HEADS].astype(f32)
     decays = jnp.broadcast_to(decays[:, :, :, None], (count, 1, SSM_HEADS, HEAD_DIM))
     decays = decays.reshape(count, 1, INNER)
     grow = by_block(jnp.exp(cumulative))
@@ -347,13 +338,13 @@
     values, bc, state = conv_state(xbc, tail, conv_weight, weight_end)
 
     held = exchange(state.reshape(count, STATE_DIM // count, INNER))
+    intra_rows = intra(values, bc, cum2, gap2, gain)
+    held, intra_rows = lax.optimization_barrier((held, intra_rows))
     initial = exchange(relay_select(parent_slot, held, decays)).reshape(STATE_DIM, INNER)
 
-    pairs = exchange(pick_pairs(parent_slot, held_pairs))
-    parent_pairs = pairs[:, 0].reshape(rows, -1)
-    grand_pairs = pairs[:, 1].reshape(rows, -1)
-    attended = attend(depth[None], queries, keys_values, parent_pairs, grand_pairs)
-    intra_rows = intra(values, bc, cum2, gap2, gain)
+    lineage = jnp.stack([depth, my_parent, my_grand])
+    attended = attend(lineage, queries, keys_values, all_pairs)
+    attended, intra_rows = lax.optimization_barrier((attended, intra_rows))
     return (finish(intra_rows, bc, initial, grow), attended)
 
 

time: 209 us -> 237 us (1.13)
  waiting for transfers between devices: 60.8 us -> 140 us
  blocking collectives: 56.7 us -> 0 us
  between operations: 4.82 us -> 18.2 us
  starting transfers between devices: 23.2 us -> 9.85 us
  other arithmetic: 0.13 us -> 6.91 us
  Pallas kernels: 53.8 us -> 49.7 us
    all_gather x2 -> x0, blocking collectives: 56.7 us -> none  [the longest x1 34.3 us: on_device(): decays = lax.all_gather(jnp.exp(last), 'branch')]
    all_to_all x4 -> x2, waiting for transfers between devices: 60.8 us -> 101 us  [exchange(): lax.all_to_all(rows, 'branch', split_axis=0, concat_axis=0, tiled=True)]
    all_gather x0 -> x2, waiting for transfers between devices: none -> 38.4 us  [the longest x1 38.4 us: on_device(): lax.all_gather(jnp.concatenate([xbc[rows - taps:], extra]), 'branch')]
    all_to_all x4 -> x2, starting transfers between devices: 23.2 us -> 9.77 us  [exchange(): lax.all_to_all(rows, 'branch', split_axis=0, concat_axis=0, tiled=True)]
    pallas_call x1 -> x0, Pallas kernels: 5.59 us -> none  [pick_pairs(): pl.pallas_call(pick_kernel, grid_spec=pltpu.PrefetchScalarGridSpec(num_sc...]
    unnamed x23 -> x18, local copies, waits for them, and re-layouts: 4.24 us -> 5.27 us
  transfers between devices with their start and end apart: 4 -> 4, of which waited for: 2 -> 3; matrix products, arithmetic and copies ran while one was open for 3% -> 3% of each run, Pallas kernels for 21% -> 17%
where the time goes in v2:
time: 237 us; the launch traced here: 236 us
  waiting for transfers between devices  140 us (59%)
  Pallas kernels  49.7 us (21%)
  between operations  18.2 us (8%)
  local copies, waits for them, and re-layouts  10.6 us (4%)
  starting transfers between devices  9.85 us (4%)
  other arithmetic  6.91 us (3%)
    all_to_all x2, waiting for transfers between devices, exchange(): lax.all_to_all(rows, 'branch', split_axis=0, concat_axis=0, tiled=True)  101 us
    all_gather x1, waiting for transfers between devices, on_device(): lax.all_gather(jnp.concatenate([xbc[rows - taps:], extra]), 'branch')  38.4 us
    pallas_call x1, Pallas kernels, attend(): pl.pallas_call(attend_kernel, grid_spec=pltpu.PrefetchScalarGridSpec(num_...  15.6 us
    pallas_call x1, Pallas kernels, conv_state(): pl.pallas_call(conv_state_kernel, grid=(steps,), in_specs=[pl.BlockSpec((...  10.8 us
    pallas_call x1, Pallas kernels, finish(): pl.pallas_call(finish_kernel, grid=(steps,), in_specs=[pl.BlockSpec((rows...  10.2 us
    pallas_call x1, Pallas kernels, intra(): pl.pallas_call(intra_kernel, grid=(INNER // COLS,), in_specs=[wide, pl.Bl...  9.82 us
    all_to_all x2, starting transfers between devices, exchange(): lax.all_to_all(rows, 'branch', split_axis=0, concat_axis=0, tiled=True)  9.77 us
    unnamed x18, local copies, waits for them, and re-layouts  5.27 us
  transfers between devices with their start and end apart: 4, of which 3 were waited for; matrix products, arithmetic and copies ran while one was open for 3% of the time, Pallas kernels for 17%

profile of v2, /device:TPU:13, one launch (start us, length us, event | category | flops | bytes accessed | tf_op | source)
XLA Modules:
  0.0 235.9 jit_solution(11103340824363220769)
XLA Ops:
  7.2 0.0 copy-start.4
  7.2 0.0 all-gather.8.cloned.1.call-start
  7.2 0.7 neg.5
  7.9 1.1 fusion
  9.0 0.2 slice_reduce_fusion
  9.2 1.6 multiply_bitcast_fusion
  10.8 0.7 reduce-precision_convert_fusion
  11.5 0.1 fusion.5
  11.6 0.9 slice.15
  12.5 0.7 maximum_bitcast_fusion
  13.2 0.0 all-gather.8.cloned.1.call-update
  13.3 0.0 all-gather.6.cloned.1.call-start
  13.3 38.4 %all-gather.8.cloned.1.call-done = bf16[16,4,8448]{2,1,0:T(4,128)(2,1)} async-done(((bf16[1,4,8448]{2,1,0:T(4,128)(2,1)}), bf16[16,4,8448]{2,1,0:T(4,128)(2,1)}) %all-gather.8.cloned.1.call-update) | async-done | bytes 1081360 | tf_op jit(solution)/shard_map/all_gather | solution.py:322
  51.7 0.0 all-gather.6.cloned.1.call-update
  51.8 1.3 dynamic_slice.10
  55.1 0.3 copy.14
  56.1 0.9 select_bitcast_fusion
  57.1 0.0 copy-done.4
  57.1 10.8 %shard_map.96 = (bf16[256,8192]{1,0:T(8,128)(2,1)}, bf16[256,256]{1,0:T(8,128)(2,1)S(1)}, bf16[128,8192]{1,0:T(8,128)(2,1)}) custom-call(bf16[256,8448]{1,0:T(8,128)(2,1)} %bc_ref.1, bf16[256,8448]{1,0:T(8,128)(2,1)} %bc_ref.1, f32[8,8448]{1,0:T(8,128)S(1)} %concatenate.12.tail_ref.tail_bc_ref, f32[8,8448]{1,0:T(8,128)S(1)} %concatenate.12.tail_ref.tail_bc_ref, ...), custom_call_target="tpu_custom_call" | custom-call | flops 600000000 | bytes 11000000 | tf_op jit(solution)/shard_map/pallas_call | solution.py:75
  67.9 0.0 copy-start.7
  67.9 0.0 copy-start.8
  67.9 5.4 %all-to-all-start = ((bf16[16,8,8192]{2,1,0:T(8,128)(2,1)}), bf16[16,8,8192]{2,1,0:T(8,128)(2,1)S(1)}, u32[]{:S(2)}, u32[]{:S(2)}) async-start(bf16[16,8,8192]{2,1,0:T(8,128)(2,1)} %bitcast.8), calls=%async_computation | async-start | bytes 4194304 | tf_op jit(solution)/shard_map/all_to_all | solution.py:300
  73.3 0.0 copy-done.7
  73.3 0.3 copy.15
  73.7 0.0 copy-done.8
  73.7 0.1 broadcast_in_dim.29
  73.7 0.0 copy-start.5
  73.7 9.8 %shard_map.97.intra_ref = f32[256,8192]{1,0:T(8,128)} custom-call(bf16[256,8192]{1,0:T(8,128)(2,1)} %get-tuple-element.14.values_ref, bf16[256,256]{1,0:T(8,128)(2,1)S(1)} %get-tuple-element.15.bc_ref.c_ref, f32[8,256,8]{2,1,0:T(8,128)S(1)} %bitcast.27, f32[64,256]{1,0:T(8,128)S(1)} %get-tuple-element.20.gap_ref, f32[1,8192]{1,0:T(1,128)S(1)} %bitcast.30), custom_call_target="tpu_custom_call" | custom-call | flops 1100000000 | bytes 12600000 | tf_op jit(solution)/shard_map/pallas_call | solution.py:221
  83.6 0.9 convert_add_fusion
  84.4 75.4 %all-to-all-done.held_ref = bf16[16,8,8192]{2,1,0:T(8,128)(2,1)S(1)} async-done(((bf16[16,8,8192]{2,1,0:T(8,128)(2,1)}), bf16[16,8,8192]{2,1,0:T(8,128)(2,1)S(1)}, u32[]{:S(2)}, u32[]{:S(2)}) %all-to-all-start) | async-done | bytes 2097184 | tf_op jit(solution)/shard_map/all_to_all | solution.py:300
  159.9 0.0 copy-start.6
  159.9 0.2 broadcast_in_dim.31
  160.1 1.1 copy-done.6
  161.2 0.0 copy-done.5
  161.2 3.4 %shard_map.98 = bf16[16,8,8192]{2,1,0:T(8,128)(2,1)S(1)} custom-call(s32[16]{0:T(128)S(1)} %copy-done.5, bf16[16,8,8192]{2,1,0:T(8,128)(2,1)} %copy-done.6, f32[16,1,8192]{2,1,0:T(1,128)S(1)} %bitcast.29), custom_call_target="tpu_custom_call" | custom-call | flops 4000000 | bytes 5000000 | tf_op jit(solution)/shard_map/pallas_call | solution.py:119
  164.6 0.0 copy-start
  164.6 1.3 copy-done
  165.9 0.0 copy-start.1
  165.9 4.4 %all-to-all-start.1 = ((bf16[16,8,8192]{2,1,0:T(8,128)(2,1)}), bf16[16,8,8192]{2,1,0:T(8,128)(2,1)S(1)}, u32[]{:S(2)}, u32[]{:S(2)}) async-start(bf16[16,8,8192]{2,1,0:T(8,128)(2,1)} %copy-done), calls=%async_computation.1 | async-start | bytes 4194304 | tf_op jit(solution)/shard_map/all_to_all | solution.py:300
  170.3 0.6 dynamic_slice.11
  172.2 1.3 copy.16
  173.5 1.4 pad_add_fusion.lineage
  174.9 0.0 all-gather.6.cloned.1.call-done
  174.9 0.0 copy-done.1
  174.9 0.0 copy-start.3
  174.9 1.6 copy-done.3
  176.5 15.6 %shard_map.95 = bf16[256,4096]{1,0:T(8,128)(2,1)} custom-call(s32[3]{0:T(128)S(1)} %pad_add_fusion.lineage, bf16[256,4096]{1,0:T(8,128)(2,1)S(1)} %copy-done.3, bf16[256,1024]{1,0:T(8,128)(2,1)S(1)} %copy-done.1, bf16[256,1024]{1,0:T(8,128)(2,1)S(1)} %copy-done.1, bf16[16,256,1024]{2,1,0:T(8,128)(2,1)} %bitcast.31, bf16[16,256,1024]{2,1,0:T(8,128)(2,1)} %bitcast.32, ...), custom_call_target="tpu_custom_call" | custom-call | flops 3300000000 | bytes 6000000 | tf_op jit(solution)/shard_map/pallas_call | solution.py:183
  192.0 25.6 %all-to-all-done.1 = bf16[16,8,8192]{2,1,0:T(8,128)(2,1)S(1)} async-done(((bf16[16,8,8192]{2,1,0:T(8,128)(2,1)}), bf16[16,8,8192]{2,1,0:T(8,128)(2,1)S(1)}, u32[]{:S(2)}, u32[]{:S(2)}) %all-to-all-start.1) | async-done | bytes 2097184 | tf_op jit(solution)/shard_map/all_to_all | solution.py:300
  217.7 0.0 copy-start.2
  217.7 1.2 copy-done.2
  218.9 10.2 %shard_map.99 = bf16[256,8192]{1,0:T(8,128)(2,1)} custom-call(f32[256,8192]{1,0:T(8,128)} %shard_map.97.intra_ref, bf16[256,256]{1,0:T(8,128)(2,1)S(1)} %get-tuple-element.15.bc_ref.c_ref, bf16[128,8192]{1,0:T(8,128)(2,1)S(1)} %bitcast.25, f32[8,256,8]{2,1,0:T(8,128)S(1)} %bitcast.28), custom_call_target="tpu_custom_call" | custom-call | flops 600000000 | bytes 14600000 | tf_op jit(solution)/shard_map/pallas_call | solution.py:268
  (2 shorter events, 0.1 us)
Async XLA Ops:
  7.2 49.9 %copy-start.4 = (f32[4,8448]{1,0:T(4,128)S(1)}, f32[4,8448]{1,0:T(4,128)}, u32[]{:S(2)}) copy-start(f32[4,8448]{1,0:T(4,128)} %w_bc_ref.1) | copy-start | bytes 405508
  7.2 44.6 %all-gather.8.cloned.1.call-start = ((), (), s32[]{:S(2)}) async-start(), calls=%async_computation.3 | async-start | bytes 1148928 | tf_op jit(solution)/shard_map/all_gather | solution.py:322
  13.3 161.6 %all-gather.6.cloned.1.call-start = ((), (), s32[]{:S(2)}) async-start(), calls=%async_computation.2 | async-start | bytes 8912896 | tf_op jit(solution)/shard_map/all_gather | solution.py:324
  67.9 5.4 %copy-start.7 = (f32[256,8,8]{0,2,1:T(8,128)S(1)}, f32[256,8,8]{0,2,1:T(8,128)}, u32[]{:S(2)}) copy-start(f32[256,8,8]{0,2,1:T(8,128)} %get-tuple-element.24) | copy-start | bytes 196612
  67.9 5.7 %copy-start.8 = (f32[64]{0:T(128)S(1)}, f32[64]{0:T(128)}, u32[]{:S(2)}) copy-start(f32[64]{0:T(128)} %param.14) | copy-start | bytes 772
  67.9 92.0 %all-to-all-start = ((bf16[16,8,8192]{2,1,0:T(8,128)(2,1)}), bf16[16,8,8192]{2,1,0:T(8,128)(2,1)S(1)}, u32[]{:S(2)}, u32[]{:S(2)}) async-start(bf16[16,8,8192]{2,1,0:T(8,128)(2,1)} %bitcast.8), calls=%async_computation | async-start | bytes 4194304 | tf_op jit(solution)/shard_map/all_to_all | solution.py:300
  73.7 87.5 %copy-start.5 = (s32[16]{0:T(128)S(1)}, s32[16]{0:T(128)}, u32[]{:S(2)}) copy-start(s32[16]{0:T(128)} %parents.1) | copy-start | bytes 196
  159.9 1.3 copy-start.6
  164.6 1.3 copy-start
  165.9 9.0 %copy-start.1 = (bf16[256,1024]{1,0:T(8,128)(2,1)S(1)}, bf16[256,1024]{1,0:T(8,128)(2,1)}, u32[]{:S(2)}) copy-start(bf16[256,1024]{1,0:T(8,128)(2,1)} %vo.1) | copy-start | bytes 1572868
  165.9 51.8 %all-to-all-start.1 = ((bf16[16,8,8192]{2,1,0:T(8,128)(2,1)}), bf16[16,8,8192]{2,1,0:T(8,128)(2,1)S(1)}, u32[]{:S(2)}, u32[]{:S(2)}) async-start(bf16[16,8,8192]{2,1,0:T(8,128)(2,1)} %copy-done), calls=%async_computation.1 | async-start | bytes 4194304 | tf_op jit(solution)/shard_map/all_to_all | solution.py:300
  174.9 1.6 copy-start.3
  217.7 1.2 copy-start.2
Sparse Core Ops, SparseCore 0:
  13.4 38.3 all-gather.7
  53.9 104.9 all-gather.5

commit v3 on v1

--- a/solution.py
+++ b/solution.py
@@ -134,11 +134,13 @@
 
 
 def pick_kernel(parents, held_ref, sent_ref):
-    slot = pl.program_id(0)
-    parent = parents[slot]
-    grand = parents[parent]
-    sent_ref[0, 0] = held_ref[parent]
-    sent_ref[0, 1] = held_ref[grand]
+    def one(slot, carry):
+        parent = parents[slot]
+        sent_ref[slot, 0] = held_ref[parent]
+        sent_ref[slot, 1] = held_ref[parents[parent]]
+        return carry
+
+    lax.fori_loop(0, held_ref.shape[0], one, 0)
 
 
 def pick_pairs(parents, held):
@@ -147,9 +149,9 @@
         pick_kernel,
         grid_spec=pltpu.PrefetchScalarGridSpec(
             num_scalar_prefetch=1,
-            grid=(count,),
+            grid=(1,),
             in_specs=[pl.BlockSpec((count, rows, cols), lambda i, p: (0, 0, 0))],
-            out_specs=pl.BlockSpec((1, 2, rows, cols), lambda i, p: (i, 0, 0, 0)),
+            out_specs=pl.BlockSpec((count, 2, rows, cols), lambda i, p: (0, 0, 0, 0)),
         ),
         out_shape=jax.ShapeDtypeStruct((count, 2, rows, cols), bf16),
         compiler_params=params(),
@@ -327,13 +329,21 @@
     is_root = my_parent == me
     depth = jnp.where(is_root, 0, jnp.where(my_grand == my_parent, 1, 2)).astype(jnp.int32)
 
-    tails = lax.all_gather(xbc[rows - taps :], "branch")
-    held_pairs = exchange(keys_values.reshape(count, rows // count, -1))
-
     cumulative = prefix_sum(-decay_rate[None, :] * step_size)
     last = cumulative[-1:]
     weight_end = by_block(jnp.exp(last - cumulative) * step_size)
-    decays = lax.all_gather(jnp.exp(last), "branch")
+    fall = jnp.exp(-decay_rate * jnp.sum(step_size, axis=0))
+    high = lax.reduce_precision(fall, 8, 7)
+    parts = jnp.concatenate([high, fall - high]).astype(bf16)
+    parts = jnp.broadcast_to(parts[None], (taps, parts.shape[0]))
+    sent = jnp.concatenate([xbc[rows - taps :], parts], axis=1)
+    gathered = lax.all_gather(sent, "branch")
+    held_pairs = exchange(keys_values.reshape(count, rows // count, -1))
+    sent_pairs = pick_pairs(parent_slot, held_pairs)
+    width = xbc.shape[1]
+    tails = gathered[:, :, :width]
+    decays = gathered[:, :1, width : width + SSM_HEADS].astype(f32)
+    decays += gathered[:, :1, width + SSM_HEADS :].astype(f32)
     decays = jnp.broadcast_to(decays[:, :, :, None], (count, 1, SSM_HEADS, HEAD_DIM))
     decays = decays.reshape(count, 1, INNER)
     grow = by_block(jnp.exp(cumulative))
@@ -344,16 +354,20 @@
     tail = lax.dynamic_index_in_dim(tails, my_parent, 0, keepdims=False).astype(f32)
     tail = jnp.where(is_root, 0.0, tail)
     tail = jnp.concatenate([jnp.zeros((8 - taps, tail.shape[1]), f32), tail], axis=0)
+    tail, sent_pairs = lax.optimization_barrier((tail, sent_pairs))
+    pairs = exchange(sent_pairs)
     values, bc, state = conv_state(xbc, tail, conv_weight, weight_end)
 
+    state, pairs = lax.optimization_barrier((state, pairs))
     held = exchange(state.reshape(count, STATE_DIM // count, INNER))
+    intra_rows = intra(values, bc, cum2, gap2, gain)
+    held, intra_rows = lax.optimization_barrier((held, intra_rows))
     initial = exchange(relay_select(parent_slot, held, decays)).reshape(STATE_DIM, INNER)
 
-    pairs = exchange(pick_pairs(parent_slot, held_pairs))
     parent_pairs = pairs[:, 0].reshape(rows, -1)
     grand_pairs = pairs[:, 1].reshape(rows, -1)
     attended = attend(depth[None], queries, keys_values, parent_pairs, grand_pairs)
-    intra_rows = intra(values, bc, cum2, gap2, gain)
+    attended, intra_rows = lax.optimization_barrier((attended, intra_rows))
     return (finish(intra_rows, bc, initial, grow), attended)
 
 

time: 209 us -> 196 us (0.938)
  blocking collectives: 56.7 us -> 20.8 us
  waiting for transfers between devices: 60.8 us -> 78.2 us
  Pallas kernels: 53.8 us -> 49.9 us
  local copies, waits for them, and re-layouts: 8.68 us -> 12.1 us
  other arithmetic: 0.13 us -> 3.41 us
    all_gather x2 -> x1, blocking collectives: 56.7 us -> 20.8 us  [on_device(): gathered = lax.all_gather(sent, 'branch')]
    all_to_all x4, waiting for transfers between devices: 60.8 us -> 78.2 us  [exchange(): lax.all_to_all(rows, 'branch', split_axis=0, concat_axis=0, tiled=True)]
    pallas_call x1, Pallas kernels: 5.59 us -> 1.7 us  [pick_pairs(): pl.pallas_call(pick_kernel, grid_spec=pltpu.PrefetchScalarGridSpec(num_sc...]
    unnamed x23 -> x18, local copies, waits for them, and re-layouts: 4.24 us -> 6.1 us
  transfers between devices with their start and end apart: 4 -> 4, of which waited for: 2 -> 3; matrix products, arithmetic and copies ran while one was open for 3% -> 5% of each run, Pallas kernels for 21% -> 18%
where the time goes in v3:
time: 196 us; the launch traced here: 195 us
  waiting for transfers between devices  78.2 us (40%)
  Pallas kernels  49.9 us (25%)
  starting transfers between devices  24.1 us (12%)
  blocking collectives  20.8 us (11%)
  local copies, waits for them, and re-layouts  12.1 us (6%)
  between operations  4.91 us (3%)
  other arithmetic  3.41 us (2%)
    all_to_all x4, waiting for transfers between devices, exchange(): lax.all_to_all(rows, 'branch', split_axis=0, concat_axis=0, tiled=True)  78.2 us
    all_to_all x4, starting transfers between devices, exchange(): lax.all_to_all(rows, 'branch', split_axis=0, concat_axis=0, tiled=True)  24.1 us
    all_gather x1, blocking collectives, on_device(): gathered = lax.all_gather(sent, 'branch')  20.8 us
    pallas_call x1, Pallas kernels, attend(): pl.pallas_call(attend_kernel, grid_spec=pltpu.PrefetchScalarGridSpec(num_...  14.2 us
    pallas_call x1, Pallas kernels, conv_state(): pl.pallas_call(conv_state_kernel, grid=(steps,), in_specs=[pl.BlockSpec((...  10.7 us
    pallas_call x1, Pallas kernels, finish(): pl.pallas_call(finish_kernel, grid=(steps,), in_specs=[pl.BlockSpec((rows...  10.2 us
    pallas_call x1, Pallas kernels, intra(): pl.pallas_call(intra_kernel, grid=(INNER // COLS,), in_specs=[wide, pl.Bl...  9.67 us
    unnamed x18, local copies, waits for them, and re-layouts  6.1 us
  transfers between devices with their start and end apart: 4, of which 3 were waited for; matrix products, arithmetic and copies ran while one was open for 5% of the time, Pallas kernels for 18%

profile of v3, /device:TPU:13, one launch (start us, length us, event | category | flops | bytes accessed | tf_op | source)
XLA Modules:
  0.0 194.6 jit_solution(7801730900554172876)
XLA Ops:
  0.6 6.6 %all-to-all-start = ((bf16[16,16,1024]{2,1,0:T(8,128)(2,1)}), bf16[16,16,1024]{2,1,0:T(8,128)(2,1)S(1)}, u32[]{:S(2)}, u32[]{:S(2)}) async-start(bf16[16,16,1024]{2,1,0:T(8,128)(2,1)} %bitcast.31), calls=%async_computation | async-start | bytes 1048576 | tf_op jit(solution)/shard_map/all_to_all | solution.py:317
  7.2 1.3 dynamic_slice.10
  10.6 0.7 neg.5
  11.2 1.1 fusion
  12.4 0.2 slice_reduce_fusion
  12.5 1.0 multiply_bitcast_fusion
  13.6 0.7 reduce-precision_convert_fusion
  14.3 0.0 copy-start.3
  14.3 1.0 slice.21
  15.2 0.1 pad_maximum_fusion
  15.4 20.8 %all-gather.1 = bf16[16,3,8576]{2,1,0:T(4,128)(2,1)S(1)} all-gather(bf16[1,3,8576]{2,1,0:T(4,128)(2,1)S(1)} %maximum_bitcast_fusion), channel_id=2, replica_groups=mesh['groups'=2,'branch'=16] {'branch'}, dimensions={0}, use_global_device_ids=true | all-gather | bytes 874752 | tf_op jit(solution)/shard_map/all_gather | solution.py:340
  36.2 0.0 copy-start.6
  36.2 1.0 copy-done.6
  37.2 0.4 slice.28
  38.3 0.0 copy-start.1
  38.3 0.0 all-to-all-done.held_ref
  38.4 0.0 copy-done.3
  38.4 1.7 shard_map.95
  40.1 7.7 %all-to-all-start.1 = ((bf16[16,2,16,1024]{3,2,1,0:T(8,128)(2,1)}), bf16[16,2,16,1024]{3,2,1,0:T(8,128)(2,1)S(1)}, u32[]{:S(2)}, u32[]{:S(2)}) async-start(bf16[16,2,16,1024]{3,2,1,0:T(8,128)(2,1)} %shard_map.95), calls=%async_computation.1 | async-start | bytes 2097152 | tf_op jit(solution)/shard_map/all_to_all | solution.py:317
  47.8 0.3 copy.14
  48.1 0.0 copy-done.1
  48.1 10.7 %shard_map.96 = (bf16[256,8192]{1,0:T(8,128)(2,1)}, bf16[256,256]{1,0:T(8,128)(2,1)S(1)}, bf16[128,8192]{1,0:T(8,128)(2,1)}) custom-call(bf16[256,8448]{1,0:T(8,128)(2,1)} %bc_ref.1, bf16[256,8448]{1,0:T(8,128)(2,1)} %bc_ref.1, f32[8,8448]{1,0:T(8,128)S(1)} %concatenate.16.tail_ref.tail_bc_ref, f32[8,8448]{1,0:T(8,128)S(1)} %concatenate.16.tail_ref.tail_bc_ref, ...), custom_call_target="tpu_custom_call" | custom-call | flops 600000000 | bytes 11000000 | tf_op jit(solution)/shard_map/pallas_call | solution.py:75
  58.8 13.9 %all-to-all-done.1 = bf16[16,2,16,1024]{3,2,1,0:T(8,128)(2,1)S(1)} async-done(((bf16[16,2,16,1024]{3,2,1,0:T(8,128)(2,1)}), bf16[16,2,16,1024]{3,2,1,0:T(8,128)(2,1)S(1)}, u32[]{:S(2)}, u32[]{:S(2)}) %all-to-all-start.1) | async-done | bytes 1048608 | tf_op jit(solution)/shard_map/all_to_all | solution.py:317
  72.7 0.0 copy-start.7
  72.7 0.0 copy-start.8
  72.7 1.1 copy-done.7
  73.7 4.9 %all-to-all-start.2 = ((bf16[16,8,8192]{2,1,0:T(8,128)(2,1)}), bf16[16,8,8192]{2,1,0:T(8,128)(2,1)S(1)}, u32[]{:S(2)}, u32[]{:S(2)}) async-start(bf16[16,8,8192]{2,1,0:T(8,128)(2,1)} %bitcast.10), calls=%async_computation.2 | async-start | bytes 4194304 | tf_op jit(solution)/shard_map/all_to_all | solution.py:317
  78.6 0.3 copy.15
  79.0 0.9 fusion.3
  79.8 0.0 copy-done.8
  79.8 0.1 broadcast_in_dim.36
  79.9 9.7 %shard_map.98.intra_ref = f32[256,8192]{1,0:T(8,128)} custom-call(bf16[256,8192]{1,0:T(8,128)(2,1)} %get-tuple-element.18.values_ref, bf16[256,256]{1,0:T(8,128)(2,1)S(1)} %get-tuple-element.19.bc_ref.c_ref, f32[8,256,8]{2,1,0:T(8,128)S(1)} %bitcast.28, f32[64,256]{1,0:T(8,128)S(1)} %get-tuple-element.26.gap_ref, f32[1,8192]{1,0:T(1,128)S(1)} %bitcast.36), custom_call_target="tpu_custom_call" | custom-call | flops 1100000000 | bytes 12600000 | tf_op jit(solution)/shard_map/pallas_call | solution.py:238
  89.6 36.5 %all-to-all-done.2.held_ref = bf16[16,8,8192]{2,1,0:T(8,128)(2,1)S(1)} async-done(((bf16[16,8,8192]{2,1,0:T(8,128)(2,1)}), bf16[16,8,8192]{2,1,0:T(8,128)(2,1)S(1)}, u32[]{:S(2)}, u32[]{:S(2)}) %all-to-all-start.2) | async-done | bytes 2097184 | tf_op jit(solution)/shard_map/all_to_all | solution.py:317
  126.1 0.0 copy-start.5
  126.1 0.2 broadcast_in_dim.38
  126.2 1.1 copy-done.5
  127.4 3.4 %shard_map.99 = bf16[16,8,8192]{2,1,0:T(8,128)(2,1)S(1)} custom-call(s32[16]{0:T(128)S(1)} %copy-done.3, bf16[16,8,8192]{2,1,0:T(8,128)(2,1)} %copy-done.5, f32[16,1,8192]{2,1,0:T(1,128)S(1)} %bitcast.30), custom_call_target="tpu_custom_call" | custom-call | flops 4000000 | bytes 5000000 | tf_op jit(solution)/shard_map/pallas_call | solution.py:119
  130.7 0.0 copy-start
  130.8 1.3 copy-done
  132.1 4.9 %all-to-all-start.3 = ((bf16[16,8,8192]{2,1,0:T(8,128)(2,1)}), bf16[16,8,8192]{2,1,0:T(8,128)(2,1)S(1)}, u32[]{:S(2)}, u32[]{:S(2)}) async-start(bf16[16,8,8192]{2,1,0:T(8,128)(2,1)} %copy-done), calls=%async_computation.3 | async-start | bytes 4194304 | tf_op jit(solution)/shard_map/all_to_all | solution.py:317
  137.0 0.6 dynamic_slice.11
  138.9 0.3 copy.16
  139.2 0.0 copy-start.2
  139.3 1.4 fusion.5
  140.6 0.0 copy-done.2
  140.6 0.0 copy-start.4
  140.6 1.6 copy-done.4
  142.2 14.2 %shard_map.97 = bf16[256,4096]{1,0:T(8,128)(2,1)} custom-call(s32[1]{0:T(128)} %bitcast.2.depth_ref, bf16[256,4096]{1,0:T(8,128)(2,1)S(1)} %copy-done.4, bf16[256,1024]{1,0:T(8,128)(2,1)S(1)} %copy-done.2, bf16[256,1024]{1,0:T(8,128)(2,1)S(1)} %copy-done.2, bf16[256,1024]{1,0:T(8,128)(2,1)S(1)} %bitcast.34, bf16[256,1024]{1,0:T(8,128)(2,1)S(1)} %bitcast.35, ...), custom_call_target="tpu_custom_call" | custom-call | flops 3300000000 | bytes 6000000 | tf_op jit(solution)/shard_map/pallas_call | solution.py:200
  156.5 27.9 %all-to-all-done.3 = bf16[16,8,8192]{2,1,0:T(8,128)(2,1)S(1)} async-done(((bf16[16,8,8192]{2,1,0:T(8,128)(2,1)}), bf16[16,8,8192]{2,1,0:T(8,128)(2,1)S(1)}, u32[]{:S(2)}, u32[]{:S(2)}) %all-to-all-start.3) | async-done | bytes 2097184 | tf_op jit(solution)/shard_map/all_to_all | solution.py:317
  184.4 10.2 %shard_map.100 = bf16[256,8192]{1,0:T(8,128)(2,1)} custom-call(f32[256,8192]{1,0:T(8,128)} %shard_map.98.intra_ref, bf16[256,256]{1,0:T(8,128)(2,1)S(1)} %get-tuple-element.19.bc_ref.c_ref, bf16[128,8192]{1,0:T(8,128)(2,1)S(1)} %bitcast.26, f32[8,256,8]{2,1,0:T(8,128)S(1)} %bitcast.29), custom_call_target="tpu_custom_call" | custom-call | flops 600000000 | bytes 14600000 | tf_op jit(solution)/shard_map/pallas_call | solution.py:285
  (3 shorter events, 0.1 us)
Async XLA Ops:
  0.6 37.7 %all-to-all-start = ((bf16[16,16,1024]{2,1,0:T(8,128)(2,1)}), bf16[16,16,1024]{2,1,0:T(8,128)(2,1)S(1)}, u32[]{:S(2)}, u32[]{:S(2)}) async-start(bf16[16,16,1024]{2,1,0:T(8,128)(2,1)} %bitcast.31), calls=%async_computation | async-start | bytes 1048576 | tf_op jit(solution)/shard_map/all_to_all | solution.py:317
  14.3 24.1 %copy-start.3 = (s32[16]{0:T(128)S(1)}, s32[16]{0:T(128)}, u32[]{:S(2)}) copy-start(s32[16]{0:T(128)} %parents.3) | copy-start | bytes 196
  36.2 1.0 copy-start.6
  38.3 9.8 %copy-start.1 = (f32[4,8448]{1,0:T(4,128)S(1)}, f32[4,8448]{1,0:T(4,128)}, u32[]{:S(2)}) copy-start(f32[4,8448]{1,0:T(4,128)} %w_bc_ref.1) | copy-start | bytes 405508
  40.1 32.6 %all-to-all-start.1 = ((bf16[16,2,16,1024]{3,2,1,0:T(8,128)(2,1)}), bf16[16,2,16,1024]{3,2,1,0:T(8,128)(2,1)S(1)}, u32[]{:S(2)}, u32[]{:S(2)}) async-start(bf16[16,2,16,1024]{3,2,1,0:T(8,128)(2,1)} %shard_map.95), calls=%async_computation.1 | async-start | bytes 2097152 | tf_op jit(solution)/shard_map/all_to_all | solution.py:317
  72.7 1.1 copy-start.7
  72.7 7.2 %copy-start.8 = (f32[64]{0:T(128)S(1)}, f32[64]{0:T(128)}, u32[]{:S(2)}) copy-start(f32[64]{0:T(128)} %param.14) | copy-start | bytes 772
  73.7 52.3 %all-to-all-start.2 = ((bf16[16,8,8192]{2,1,0:T(8,128)(2,1)}), bf16[16,8,8192]{2,1,0:T(8,128)(2,1)S(1)}, u32[]{:S(2)}, u32[]{:S(2)}) async-start(bf16[16,8,8192]{2,1,0:T(8,128)(2,1)} %bitcast.10), calls=%async_computation.2 | async-start | bytes 4194304 | tf_op jit(solution)/shard_map/all_to_all | solution.py:317
  126.1 1.3 copy-start.5
  130.7 1.3 copy-start
  132.1 52.3 %all-to-all-start.3 = ((bf16[16,8,8192]{2,1,0:T(8,128)(2,1)}), bf16[16,8,8192]{2,1,0:T(8,128)(2,1)S(1)}, u32[]{:S(2)}, u32[]{:S(2)}) async-start(bf16[16,8,8192]{2,1,0:T(8,128)(2,1)} %copy-done), calls=%async_computation.3 | async-start | bytes 4194304 | tf_op jit(solution)/shard_map/all_to_all | solution.py:317
  139.2 1.4 copy-start.2
  140.6 1.6 copy-start.4

commit v4 on v3

--- a/solution.py
+++ b/solution.py
@@ -335,15 +335,17 @@
     fall = jnp.exp(-decay_rate * jnp.sum(step_size, axis=0))
     high = lax.reduce_precision(fall, 8, 7)
     parts = jnp.concatenate([high, fall - high]).astype(bf16)
-    parts = jnp.broadcast_to(parts[None], (taps, parts.shape[0]))
-    sent = jnp.concatenate([xbc[rows - taps :], parts], axis=1)
-    gathered = lax.all_gather(sent, "branch")
-    held_pairs = exchange(keys_values.reshape(count, rows // count, -1))
+    pairs = keys_values.reshape(count, rows // count, -1)
+    share, width = taps * xbc.shape[1] // count, pairs.shape[2]
+    parts = jnp.broadcast_to(parts[None], (count, parts.shape[0]))
+    extra = jnp.concatenate([xbc[rows - taps :].reshape(count, share), parts], axis=1)
+    more = -(-extra.shape[1] // width)
+    extra = jnp.pad(extra, ((0, 0), (0, more * width - extra.shape[1])))
+    held_pairs = exchange(jnp.concatenate([pairs, extra.reshape(count, more, width)], axis=1))
     sent_pairs = pick_pairs(parent_slot, held_pairs)
-    width = xbc.shape[1]
-    tails = gathered[:, :, :width]
-    decays = gathered[:, :1, width : width + SSM_HEADS].astype(f32)
-    decays += gathered[:, :1, width + SSM_HEADS :].astype(f32)
+    decays = held_pairs[:, rows // count :].reshape(count, 1, -1)[:, :, share : share + 2 * SSM_HEADS]
+    decays = decays.astype(f32)
+    decays = decays[:, :, :SSM_HEADS] + decays[:, :, SSM_HEADS:]
     decays = jnp.broadcast_to(decays[:, :, :, None], (count, 1, SSM_HEADS, HEAD_DIM))
     decays = decays.reshape(count, 1, INNER)
     grow = by_block(jnp.exp(cumulative))
@@ -351,21 +353,20 @@
     gap2 = ((cumulative - jnp.log(step_size)) * LOG2E).T
     gain = jnp.broadcast_to(skip_gain[:, None], (SSM_HEADS, HEAD_DIM)).reshape(1, INNER)
 
-    tail = lax.dynamic_index_in_dim(tails, my_parent, 0, keepdims=False).astype(f32)
+    pairs = exchange(sent_pairs)
+    tail = pairs[:, 0, rows // count :].reshape(count, -1)[:, :share]
+    tail = tail.reshape(taps, xbc.shape[1]).astype(f32)
     tail = jnp.where(is_root, 0.0, tail)
     tail = jnp.concatenate([jnp.zeros((8 - taps, tail.shape[1]), f32), tail], axis=0)
-    tail, sent_pairs = lax.optimization_barrier((tail, sent_pairs))
-    pairs = exchange(sent_pairs)
     values, bc, state = conv_state(xbc, tail, conv_weight, weight_end)
 
-    state, pairs = lax.optimization_barrier((state, pairs))
     held = exchange(state.reshape(count, STATE_DIM // count, INNER))
     intra_rows = intra(values, bc, cum2, gap2, gain)
     held, intra_rows = lax.optimization_barrier((held, intra_rows))
     initial = exchange(relay_select(parent_slot, held, decays)).reshape(STATE_DIM, INNER)
 
-    parent_pairs = pairs[:, 0].reshape(rows, -1)
-    grand_pairs = pairs[:, 1].reshape(rows, -1)
+    parent_pairs = pairs[:, 0, : rows // count].reshape(rows, -1)
+    grand_pairs = pairs[:, 1, : rows // count].reshape(rows, -1)
     attended = attend(depth[None], queries, keys_values, parent_pairs, grand_pairs)
     attended, intra_rows = lax.optimization_barrier((attended, intra_rows))
     return (finish(intra_rows, bc, initial, grow), attended)

time: 196 us -> 202 us (1.031)
  waiting for transfers between devices: 78.2 us -> 87.5 us
  starting transfers between devices: 24.1 us -> 15 us
  blocking collectives: 20.8 us -> 25.6 us
  local copies, waits for them, and re-layouts: 12.1 us -> 14.5 us
    all_to_all x0 -> x1, blocking collectives: none -> 25.6 us  [exchange(): lax.all_to_all(rows, 'branch', split_axis=0, concat_axis=0, tiled=True)]
    all_gather x1 -> x0, blocking collectives: 20.8 us -> none  [on_device(): gathered = lax.all_gather(sent, 'branch')]
    all_to_all x4 -> x3, waiting for transfers between devices: 78.2 us -> 87.5 us  [exchange(): lax.all_to_all(rows, 'branch', split_axis=0, concat_axis=0, tiled=True)]
    all_to_all x4 -> x3, starting transfers between devices: 24.1 us -> 15 us  [exchange(): lax.all_to_all(rows, 'branch', split_axis=0, concat_axis=0, tiled=True)]
    pallas_call x0 -> x1, local copies, waits for them, and re-layouts: none -> 2.23 us  [pick_pairs(): pl.pallas_call(pick_kernel, grid_spec=pltpu.PrefetchScalarGridSpec(num_sc...]
    slice x3 -> x4, local copies, waits for them, and re-layouts: 2.7 us -> 4.84 us  [the longest x1 3.46 us: on_device(): grand_pairs = pairs[:, 1, :rows // count].reshape(rows, -1)]
    unnamed x18 -> x21, local copies, waits for them, and re-layouts: 6.1 us -> 4.41 us
  transfers between devices with their start and end apart: 4 -> 3, of which waited for: 3 -> 3; matrix products, arithmetic and copies ran while one was open for 5% -> 3% of each run, Pallas kernels for 18% -> 12%
where the time goes in v4:
time: 202 us; the launch traced here: 201 us
  waiting for transfers between devices  87.5 us (43%)
  Pallas kernels  48.6 us (24%)
  blocking collectives  25.6 us (13%)
  starting transfers between devices  15 us (7%)
  local copies, waits for them, and re-layouts  14.5 us (7%)
  between operations  4.39 us (2%)
  other arithmetic  4.34 us (2%)
    all_to_all x3, waiting for transfers between devices, exchange(): lax.all_to_all(rows, 'branch', split_axis=0, concat_axis=0, tiled=True)  87.5 us
    all_to_all x1, blocking collectives, exchange(): lax.all_to_all(rows, 'branch', split_axis=0, concat_axis=0, tiled=True)  25.6 us
    all_to_all x3, starting transfers between devices, exchange(): lax.all_to_all(rows, 'branch', split_axis=0, concat_axis=0, tiled=True)  15 us
    pallas_call x1, Pallas kernels, attend(): pl.pallas_call(attend_kernel, grid_spec=pltpu.PrefetchScalarGridSpec(num_...  14.2 us
    pallas_call x1, Pallas kernels, conv_state(): pl.pallas_call(conv_state_kernel, grid=(steps,), in_specs=[pl.BlockSpec((...  10.4 us
    pallas_call x1, Pallas kernels, finish(): pl.pallas_call(finish_kernel, grid=(steps,), in_specs=[pl.BlockSpec((rows...  10.2 us
    pallas_call x1, Pallas kernels, intra(): pl.pallas_call(intra_kernel, grid=(INNER // COLS,), in_specs=[wide, pl.Bl...  9.71 us
    unnamed x21, local copies, waits for them, and re-layouts  4.41 us
  transfers between devices with their start and end apart: 3, of which 3 were waited for; matrix products, arithmetic and copies ran while one was open for 3% of the time, Pallas kernels for 12%

profile of v4, /device:TPU:13, one launch (start us, length us, event | category | flops | bytes accessed | tf_op | source)
XLA Modules:
  0.0 201.0 jit_solution(9223239131531143271)
XLA Ops:
  0.6 0.0 copy-start.4
  0.6 0.7 neg.5
  1.3 1.1 fusion
  2.4 0.2 slice_reduce_fusion.1
  2.6 1.6 multiply_bitcast_fusion
  4.2 0.7 reduce-precision_convert_fusion
  4.9 0.9 slice.30
  5.8 0.1 reshape.65
  6.0 0.1 pad_maximum_fusion.2
  6.1 1.2 pad_maximum_fusion
  7.3 25.6 %all_to_all.20.held_ref = bf16[16,18,1024]{2,1,0:T(8,128)(2,1)S(1)} all-to-all(bf16[16,18,1024]{2,1,0:T(8,128)(2,1)S(1)} %pad_maximum_fusion), channel_id=1, replica_groups=mesh['groups'=2,'branch'=16] {'branch'}, dimensions={0} | all-to-all | bytes 1179648 | tf_op jit(solution)/shard_map/all_to_all | solution.py:317
  32.8 0.0 copy-done.4
  32.8 0.7 shard_map.95
  33.6 2.2 %copy.18 = bf16[16,2,18,1024]{3,1,2,0:T(2,128)(2,1)} copy(bf16[16,2,18,1024]{3,2,1,0:T(8,128)(2,1)S(1)} %shard_map.95) | data formatting | bytes 2359296 | tf_op jit(solution)/shard_map/pallas_call | solution.py:148
  35.8 0.0 copy-start.2
  35.8 5.1 %all-to-all-start.1 = ((bf16[16,2,18,1024]{3,1,2,0:T(2,128)(2,1)}), bf16[16,2,18,1024]{3,1,2,0:T(2,128)(2,1)S(1)}, u32[]{:S(2)}, u32[]{:S(2)}) async-start(bf16[16,2,18,1024]{3,1,2,0:T(2,128)(2,1)} %copy.18), calls=%async_computation.1 | async-start | bytes 2359296 | tf_op jit(solution)/shard_map/all_to_all | solution.py:317
  40.9 0.6 dynamic_slice.6
  42.1 0.3 copy.21
  42.4 26.3 %all-to-all-done.1 = bf16[16,2,18,1024]{3,1,2,0:T(2,128)(2,1)S(1)} async-done(((bf16[16,2,18,1024]{3,1,2,0:T(2,128)(2,1)}), bf16[16,2,18,1024]{3,1,2,0:T(2,128)(2,1)S(1)}, u32[]{:S(2)}, u32[]{:S(2)}) %all-to-all-start.1) | async-done | bytes 1179680 | tf_op jit(solution)/shard_map/all_to_all | solution.py:317
  68.7 0.0 copy-start.6
  68.7 0.4 slice_reduce_fusion
  69.1 0.2 select_n.31
  69.3 0.0 copy-done.2
  69.3 10.4 %shard_map.97 = (bf16[256,8192]{1,0:T(8,128)(2,1)}, bf16[256,256]{1,0:T(8,128)(2,1)S(1)}, bf16[128,8192]{1,0:T(8,128)(2,1)S(1)}) custom-call(bf16[256,8448]{1,0:T(8,128)(2,1)} %bc_ref.1, bf16[256,8448]{1,0:T(8,128)(2,1)} %bc_ref.1, f32[8,8448]{1,0:T(8,128)S(1)} %concatenate.20.tail_ref.tail_bc_ref, f32[8,8448]{1,0:T(8,128)S(1)} %concatenate.20.tail_ref.tail_bc_ref, ...), custom_call_target="tpu_custom_call" | custom-call | flops 600000000 | bytes 11000000 | tf_op jit(solution)/shard_map/pallas_call | solution.py:75
  79.7 0.0 copy-start.1
  79.7 1.3 copy-done.1
  81.0 0.0 copy-start.7
  81.0 0.0 copy-start.8
  81.0 0.0 copy-done.6
  81.0 5.0 %all-to-all-start.2 = ((bf16[16,8,8192]{2,1,0:T(8,128)(2,1)}), bf16[16,8,8192]{2,1,0:T(8,128)(2,1)}, u32[]{:S(2)}, u32[]{:S(2)}) async-start(bf16[16,8,8192]{2,1,0:T(8,128)(2,1)} %bitcast.30), calls=%async_computation.2 | async-start | bytes 4194304 | tf_op jit(solution)/shard_map/all_to_all | solution.py:317
  86.0 0.0 copy-done.7
  86.0 0.3 copy.22
  86.5 0.1 slice_convert_fusion
  86.5 0.1 fusion.3
  86.6 0.0 copy-done.8
  86.6 0.1 broadcast_in_dim.36
  86.7 9.7 %shard_map.98.intra_ref = f32[256,8192]{1,0:T(8,128)} custom-call(bf16[256,8192]{1,0:T(8,128)(2,1)} %get-tuple-element.10.values_ref, bf16[256,256]{1,0:T(8,128)(2,1)S(1)} %get-tuple-element.11.bc_ref.c_ref, f32[8,256,8]{2,1,0:T(8,128)S(1)} %bitcast.27, f32[64,256]{1,0:T(8,128)S(1)} %get-tuple-element.18.gap_ref, f32[1,8192]{1,0:T(1,128)S(1)} %bitcast.36), custom_call_target="tpu_custom_call" | custom-call | flops 1100000000 | bytes 12600000 | tf_op jit(solution)/shard_map/pallas_call | solution.py:238
  96.4 37.2 %all-to-all-done.2.held_ref = bf16[16,8,8192]{2,1,0:T(8,128)(2,1)} async-done(((bf16[16,8,8192]{2,1,0:T(8,128)(2,1)}), bf16[16,8,8192]{2,1,0:T(8,128)(2,1)}, u32[]{:S(2)}, u32[]{:S(2)}) %all-to-all-start.2) | async-done | bytes 2097184 | tf_op jit(solution)/shard_map/all_to_all | solution.py:317
  133.6 0.2 broadcast_in_dim.38
  133.8 3.4 %shard_map.99 = bf16[16,8,8192]{2,1,0:T(8,128)(2,1)S(1)} custom-call(s32[16]{0:T(128)S(1)} %copy-done.4, bf16[16,8,8192]{2,1,0:T(8,128)(2,1)} %all-to-all-done.2.held_ref, f32[16,1,8192]{2,1,0:T(1,128)S(1)} %bitcast.29), custom_call_target="tpu_custom_call" | custom-call | flops 4000000 | bytes 5000000 | tf_op jit(solution)/shard_map/pallas_call | solution.py:119
  137.1 0.0 copy-start
  137.1 1.3 copy-done
  138.5 4.9 %all-to-all-start.3 = ((bf16[16,8,8192]{2,1,0:T(8,128)(2,1)}), bf16[16,8,8192]{2,1,0:T(8,128)(2,1)S(1)}, u32[]{:S(2)}, u32[]{:S(2)}) async-start(bf16[16,8,8192]{2,1,0:T(8,128)(2,1)} %copy-done), calls=%async_computation.3 | async-start | bytes 4194304 | tf_op jit(solution)/shard_map/all_to_all | solution.py:317
  145.1 0.6 dynamic_slice.7
  146.9 0.3 copy.23
  147.2 3.5 %fusion.5 = (bf16[16,1,16,1024]{3,1,2,0:T(2,128)(2,1)S(1)}, bf16[16,1,16,1024]{3,1,2,0:T(2,128)(2,1)S(1)}) fusion(bf16[16,2,18,1024]{3,1,2,0:T(2,128)(2,1)} %copy-done.6), kind=kLoop, calls=%fused_computation.21 | loop fusion | bytes 2097152 | tf_op jit(solution)/shard_map/slice | solution.py:369
  150.7 0.0 copy-start.3
  150.7 0.0 copy-start.5
  150.7 0.2 copy.24
  150.9 0.2 copy.25
  151.1 0.7 copy-done.3
  151.7 0.7 copy-done.5
  152.5 14.2 %shard_map.96 = bf16[256,4096]{1,0:T(8,128)(2,1)} custom-call(s32[1]{0:T(128)} %bitcast.2.depth_ref, bf16[256,4096]{1,0:T(8,128)(2,1)S(1)} %copy-done.5, bf16[256,1024]{1,0:T(8,128)(2,1)S(1)} %copy-done.3, bf16[256,1024]{1,0:T(8,128)(2,1)S(1)} %copy-done.3, bf16[256,1024]{1,0:T(8,128)(2,1)S(1)} %bitcast.31, bf16[256,1024]{1,0:T(8,128)(2,1)S(1)} %bitcast.32, ...), custom_call_target="tpu_custom_call" | custom-call | flops 3300000000 | bytes 6000000 | tf_op jit(solution)/shard_map/pallas_call | solution.py:200
  166.7 24.1 %all-to-all-done.3 = bf16[16,8,8192]{2,1,0:T(8,128)(2,1)S(1)} async-done(((bf16[16,8,8192]{2,1,0:T(8,128)(2,1)}), bf16[16,8,8192]{2,1,0:T(8,128)(2,1)S(1)}, u32[]{:S(2)}, u32[]{:S(2)}) %all-to-all-start.3) | async-done | bytes 2097184 | tf_op jit(solution)/shard_map/all_to_all | solution.py:317
  190.8 10.2 %shard_map.100 = bf16[256,8192]{1,0:T(8,128)(2,1)} custom-call(f32[256,8192]{1,0:T(8,128)} %shard_map.98.intra_ref, bf16[256,256]{1,0:T(8,128)(2,1)S(1)} %get-tuple-element.11.bc_ref.c_ref, bf16[128,8192]{1,0:T(8,128)(2,1)S(1)} %bitcast.25, f32[8,256,8]{2,1,0:T(8,128)S(1)} %bitcast.28), custom_call_target="tpu_custom_call" | custom-call | flops 600000000 | bytes 14600000 | tf_op jit(solution)/shard_map/pallas_call | solution.py:285
  (8 shorter events, 0.2 us)
Async XLA Ops:
  0.6 32.2 %copy-start.4 = (s32[16]{0:T(128)S(1)}, s32[16]{0:T(128)}, u32[]{:S(2)}) copy-start(s32[16]{0:T(128)} %parents.3) | copy-start | bytes 196
  35.8 33.5 %copy-start.2 = (f32[4,8448]{1,0:T(4,128)S(1)}, f32[4,8448]{1,0:T(4,128)}, u32[]{:S(2)}) copy-start(f32[4,8448]{1,0:T(4,128)} %w_bc_ref.1) | copy-start | bytes 405508
  35.8 32.9 %all-to-all-start.1 = ((bf16[16,2,18,1024]{3,1,2,0:T(2,128)(2,1)}), bf16[16,2,18,1024]{3,1,2,0:T(2,128)(2,1)S(1)}, u32[]{:S(2)}, u32[]{:S(2)}) async-start(bf16[16,2,18,1024]{3,1,2,0:T(2,128)(2,1)} %copy.18), calls=%async_computation.1 | async-start | bytes 2359296 | tf_op jit(solution)/shard_map/all_to_all | solution.py:317
  68.7 12.3 %copy-start.6 = (bf16[16,2,18,1024]{3,1,2,0:T(2,128)(2,1)}, bf16[16,2,18,1024]{3,1,2,0:T(2,128)(2,1)S(1)}, u32[]{:S(2)}) copy-start(bf16[16,2,18,1024]{3,1,2,0:T(2,128)(2,1)S(1)} %all-to-all-done.1) | copy-start | bytes 3538948
  79.7 1.3 copy-start.1
  81.0 5.0 %copy-start.7 = (f32[256,8,8]{0,2,1:T(8,128)S(1)}, f32[256,8,8]{0,2,1:T(8,128)}, u32[]{:S(2)}) copy-start(f32[256,8,8]{0,2,1:T(8,128)} %get-tuple-element.22) | copy-start | bytes 196612
  81.0 5.6 %copy-start.8 = (f32[64]{0:T(128)S(1)}, f32[64]{0:T(128)}, u32[]{:S(2)}) copy-start(f32[64]{0:T(128)} %param.14) | copy-start | bytes 772
  81.0 52.5 %all-to-all-start.2 = ((bf16[16,8,8192]{2,1,0:T(8,128)(2,1)}), bf16[16,8,8192]{2,1,0:T(8,128)(2,1)}, u32[]{:S(2)}, u32[]{:S(2)}) async-start(bf16[16,8,8192]{2,1,0:T(8,128)(2,1)} %bitcast.30), calls=%async_computation.2 | async-start | bytes 4194304 | tf_op jit(solution)/shard_map/all_to_all | solution.py:317
  137.1 1.3 copy-start
  138.5 52.3 %all-to-all-start.3 = ((bf16[16,8,8192]{2,1,0:T(8,128)(2,1)}), bf16[16,8,8192]{2,1,0:T(8,128)(2,1)S(1)}, u32[]{:S(2)}, u32[]{:S(2)}) async-start(bf16[16,8,8192]{2,1,0:T(8,128)(2,1)} %copy-done), calls=%async_computation.3 | async-start | bytes 4194304 | tf_op jit(solution)/shard_map/all_to_all | solution.py:317
  150.7 1.0 copy-start.3
  150.7 1.8 copy-start.5
